TPU v7x, 32 devices: a whole 2x2x4 slice. The times are simulated.
32 devices in a mesh: section: 2 (over core), dp: 4 (over z), mp: 4 (over y, x).
Axes of the slice: x: 2, y: 2, z: 4, core: 2. Of those that a mesh axis runs over, the one named last changes fastest.
Arguments:
- inputs: bfloat16 [8192, 768], P(('dp', 'mp')), may hold values from -6 to 6
- cotangent: bfloat16 [8192, 768], P(('dp', 'mp')), may hold values from -6 to 6
- doc_ids: int32 [8192], P('dp'), may hold values from -1 to 3, as said below
- norm_gain: float32 [2, 768], P('section'), may hold values from 0.25 to 1.75
- norm_bias: float32 [2, 768], P('section'), may hold values from -1.5 to 1.5
- w_query: bfloat16 [2, 768, 768], P('section', 'dp', 'mp'), may hold values from -0.21875 to 0.21875
- w_key: bfloat16 [2, 768, 768], P('section', 'dp', 'mp'), may hold values from -0.21875 to 0.21875
- w_value: bfloat16 [2, 768, 768], P('section', 'dp', 'mp'), may hold values from -0.21875 to 0.21875
- inner_gain: float32 [2, 768], P('section', 'mp'), may hold values from 0.25 to 1.75
- inner_bias: float32 [2, 768], P('section', 'mp'), may hold values from -1.5 to 1.5
- w_output: bfloat16 [2, 768, 768], P('section', 'mp', 'dp'), may hold values from -0.21875 to 0.21875
- feed_gain: float32 [2, 768], P('section'), may hold values from 0.25 to 1.75
- feed_bias: float32 [2, 768], P('section'), may hold values from -1.5 to 1.5
- w_up: bfloat16 [2, 768, 3072], P('section', 'dp', 'mp'), may hold values from -0.21875 to 0.21875
- middle_gain: float32 [2, 3072], P('section', 'mp'), may hold values from 0.25 to 1.75
- middle_bias: float32 [2, 3072], P('section', 'mp'), may hold values from -1.5 to 1.5
- w_down: bfloat16 [2, 3072, 768], P('section', 'mp', 'dp'), may hold values from -0.109375 to 0.109375
Outputs:
- layer_outputs: bfloat16 [2, 8192, 768], P('section', ('dp', 'mp'))
- input_grads: bfloat16 [2, 8192, 768], P('section', ('dp', 'mp'))
- grad_norm_gain: float32 [2, 768], P('section', ('dp', 'mp'))
- grad_norm_bias: float32 [2, 768], P('section', ('dp', 'mp'))
- grad_query: float32 [2, 768, 768], P('section', 'dp', 'mp')
- grad_key: float32 [2, 768, 768], P('section', 'dp', 'mp')
- grad_value: float32 [2, 768, 768], P('section', 'dp', 'mp')
- grad_inner_gain: float32 [2, 768], P('section', ('mp', 'dp'))
- grad_inner_bias: float32 [2, 768], P('section', ('mp', 'dp'))
- grad_output: float32 [2, 768, 768], P('section', 'mp', 'dp')
- grad_feed_gain: float32 [2, 768], P('section', ('dp', 'mp'))
- grad_feed_bias: float32 [2, 768], P('section', ('dp', 'mp'))
- grad_up: float32 [2, 768, 3072], P('section', 'dp', 'mp')
- grad_middle_gain: float32 [2, 3072], P('section', ('mp', 'dp'))
- grad_middle_bias: float32 [2, 3072], P('section', ('mp', 'dp'))
- grad_down: float32 [2, 3072, 768], P('section', 'mp', 'dp')
Inputs may be any that keep to these rules, and one draw needn't show every extreme that they name: `doc_ids`: along the 1024 rows of each micro-batch document numbers never fall; padding rows (-1) come last; each micro-batch holds documents 0 to 3 and some padding, and document 2 starts within the first 256 rows and ends within the last 256 rows.
All inputs are finite; a program needn't handle non-finite values.
Results may differ from a plain program's by a relative error of at most 0.028.
Values may be sent and summed in bfloat16 or wider, within the bound.
No kernel may reach another device: no remote copies, remote signals or barrier semaphores. Data moves between devices by JAX's collectives and lax.ppermute only.
A program may use at most 192 MiB of HBM per device.

v0:
```python
from functools import partial

import jax
import jax.numpy as jnp
from jax import lax
from jax.experimental import pallas as pl
from jax.experimental.pallas import tpu as pltpu
from jax.sharding import PartitionSpec as P

D = 768
HEAD_DIM = 64
FF = 3072
MICRO = 2
LANES = 4
EPS = 1e-05
SCALE = HEAD_DIM ** (-0.5)
LOG2E = 1.4426950408889634
SQRT_HALF = 0.7071067811865476
INV_SQRT_2PI = 0.3989422804014327
BOTH = ("section", "mp")
Y_PAIRS = [[0, 2], [1, 3]]
QKV = 3 * D // LANES
UNITS = FF // LANES
TAIL = 16
F32 = jnp.float32
BF16 = jnp.bfloat16

VMEM = pl.BlockSpec(memory_space=pltpu.VMEM)
SMEM = pl.BlockSpec(memory_space=pltpu.SMEM)
ANY = pl.BlockSpec(memory_space=pl.ANY)
HBM = pl.BlockSpec(memory_space=pltpu.HBM)
PARAMS = pltpu.CompilerParams(vmem_limit_bytes=16 * 1024 * 1024)


def call(name, body, outs, ins, scratch=(), after=(), cost=None):
    count = len(ins)

    def kernel(*refs):
        body(*refs[:count], *refs[count + len(after) :])

    return pl.pallas_call(
        kernel,
        out_shape=tuple(jax.ShapeDtypeStruct(shape, kind) for shape, kind in outs),
        in_specs=[SMEM if item.ndim == 1 else VMEM for item in ins] + [ANY] * len(after),
        out_specs=(VMEM,) * len(outs),
        scratch_shapes=list(scratch),
        compiler_params=PARAMS,
        name=name,
        cost_estimate=cost or work(1, 1),
    )(*ins, *after)


def work(flops, size):
    return pl.CostEstimate(flops=int(flops), bytes_accessed=int(size), transcendentals=0)


def nn(a, b):
    return jnp.dot(a, b, preferred_element_type=F32)


def nt(a, b):
    return lax.dot_general(a, b, (((1,), (1,)), ((), ())), preferred_element_type=F32)


def tn(a, b):
    return lax.dot_general(a, b, (((0,), (0,)), ((), ())), preferred_element_type=F32)


def to_rows(*columns):
    count = columns[0].shape[0]
    lane = lax.broadcasted_iota(jnp.int32, (count, 128), 1)
    tile = jnp.zeros((count, 128), F32)
    for place, column in enumerate(columns):
        tile = jnp.where(lane == place, column, tile)
    return tile.T[:8]


def to_columns(rows):
    return jnp.concatenate([rows, jnp.zeros((120, rows.shape[1]), F32)], axis=0).T


def split_three(values):
    high = values.astype(BF16)
    rest = values - high.astype(F32)
    middle = rest.astype(BF16)
    return high, middle, (rest - middle.astype(F32)).astype(BF16)


def encode(rows):
    return jnp.concatenate(split_three(rows), axis=1)


def decode(tail):
    tail = tail.astype(F32)
    count = tail.shape[1] // 3
    return tail[:, :count] + tail[:, count : 2 * count] + tail[:, 2 * count :]


def decode_vectors(tail):
    tail = tail.astype(F32)
    return jnp.concatenate(
        [jnp.sum(tail[0:3], axis=0, keepdims=True), jnp.sum(tail[3:6], axis=0, keepdims=True)],
        axis=0,
    )


def encode_vectors(first, second):
    return jnp.concatenate(
        [*split_three(first), *split_three(second), jnp.zeros((2, first.shape[1]), BF16)], axis=0
    )


def split_norm(values):
    mean = jnp.mean(values, axis=-1, keepdims=True)
    spread = jnp.mean(values * values, axis=-1, keepdims=True) - mean * mean
    scaled = lax.rsqrt(spread + EPS)
    return (values - mean) * scaled, scaled


def norm_back(values, gain, upstream):
    normal, scaled = split_norm(values)
    inner = upstream * gain
    one = jnp.mean(inner, axis=-1, keepdims=True)
    two = jnp.mean(inner * normal, axis=-1, keepdims=True)
    back = scaled * (inner - one - normal * two)
    return (
        back,
        jnp.sum(upstream * normal, axis=0, keepdims=True),
        jnp.sum(upstream, axis=0, keepdims=True),
    )


def vector_rows(first, second):
    return jnp.concatenate([first, second, jnp.zeros((6, first.shape[1]), F32)], axis=0)


def folded_vectors(mat, gain, bias):
    rows = jnp.concatenate(
        [*split_three(gain), *split_three(bias), jnp.zeros((10, gain.shape[1]), BF16)], axis=0
    )
    folded = nt(rows, mat)
    return encode_vectors(
        jnp.sum(folded[0:3], axis=0, keepdims=True), jnp.sum(folded[3:6], axis=0, keepdims=True)
    )


def core_swap(x):
    return lax.ppermute(x, "section", [(0, 1), (1, 0)])


def x_swap(x):
    return lax.ppermute(x, "mp", [(i, i ^ 1) for i in range(LANES)])


def y_swap(x):
    return lax.ppermute(x, "mp", [(i, i ^ 2) for i in range(LANES)])


def gather_rows(own):
    far = x_swap(own)
    return own, core_swap(own), far, core_swap(far)


def pair_sum_body(first, second, out):
    rows = out.shape[0] - TAIL
    out[:rows] = (first[:rows].astype(F32) + second[:rows].astype(F32)).astype(BF16)
    half = rows + TAIL // 2
    out[rows:half] = encode(decode(first[rows:half]) + decode(second[rows:half]))
    folded = decode_vectors(first[half:]) + decode_vectors(second[half:])
    out[half:] = encode_vectors(folded[0:1], folded[1:2])


def pair_add_body(first, second, out):
    out[...] = (first[...].astype(F32) + second[...].astype(F32)).astype(BF16)


def pair_sum(far, far_mate):
    body = pair_sum_body if far.shape[0] % 256 else pair_add_body
    return call("pair_sum", body, [(far.shape, BF16)], [far, core_swap(far_mate)])[0]


def settle(own, mate, far, far_mate):
    sent = pair_sum(far, far_mate)
    return own, core_swap(mate), x_swap(sent)


def project_body(first, second, mat, out):
    size = first.shape[0]
    for place, piece in enumerate((first, second)):
        out[place * size : (place + 1) * size, :] = nn(piece[...], mat[:, :QKV]).astype(BF16)


def project(first, second, mat):
    count = 2 * first.shape[0]
    return call(
        "project",
        project_body,
        [((count, QKV), BF16)],
        [first, second, mat],
    )[0]


def split_heads(source, target, first, start, head_count):
    size = source.shape[0]
    for head in range(head_count):
        lanes = slice(first + head * HEAD_DIM, first + (head + 1) * HEAD_DIM)
        target[head, start : start + size, :] = source[:, lanes]


def attend_body(
    q_start, q_ref, near, far, labels, mat, gain, bias, o_ref, p_one, p_two, sum_ref, ks, vs
):
    head_count = QKV // (3 * HEAD_DIM)
    width = head_count * HEAD_DIM
    half = near.shape[0]
    for start, ref in ((0, near), (half, far)):
        split_heads(ref, ks, width, start, head_count)
        split_heads(ref, vs, 2 * width, start, head_count)
    out_mat = mat[:, QKV:]
    folded = folded_vectors(out_mat, gain[...], bias[...])
    size = half // 2
    key_labels = labels[0:1, :]
    for place, p_ref in enumerate((p_one, p_two)):
        rows = slice(place * size, (place + 1) * size)
        first = q_start + place * size
        allowed = to_columns(labels[:, first : first + size])[:, 0:1] == key_labels
        outs = []
        sums = []
        for head in range(head_count):
            query = q_ref[rows, head * HEAD_DIM : (head + 1) * HEAD_DIM]
            scores = jnp.where(allowed, nt(query, ks[head]), -1e30)
            peak = jnp.max(scores, axis=-1, keepdims=True)
            terms = jnp.exp2((scores - peak) * (SCALE * LOG2E))
            total = jnp.sum(terms, axis=-1, keepdims=True)
            outs.append(nn(terms.astype(BF16), vs[head]) / total)
            sums.append(peak * (SCALE * LOG2E) + jnp.log(total) * LOG2E)
        out = jnp.concatenate(outs, axis=1)
        o_ref[rows, :] = out
        lane = lax.broadcasted_iota(jnp.int32, (size, 128), 1)
        tile = jnp.zeros((size, 128), F32)
        for spot, column in enumerate(sums):
            tile = jnp.where(lane == spot, column, tile)
        sum_ref[rows, :] = tile
        p_ref[:size] = nt((out * gain[...]).astype(BF16), out_mat).astype(BF16)
        stats = to_rows(
            jnp.sum(out, axis=-1, keepdims=True), jnp.sum(out * out, axis=-1, keepdims=True)
        )
        p_ref[size : size + TAIL // 2] = encode(stats)
        p_ref[size + TAIL // 2 :] = folded


def attend(q_start, queries, near, far, labels, mat, gain, bias, after=()):
    count, keys = queries.shape[0], 2 * near.shape[0]
    heads = QKV // (3 * HEAD_DIM)
    width = heads * HEAD_DIM
    by_head = pltpu.VMEM((heads, keys, HEAD_DIM), BF16)
    payload = ((count // 2 + TAIL, D), BF16)
    return call(
        "attend",
        partial(attend_body, q_start),
        [((count, width), F32), payload, payload, ((count, 128), F32)],
        [queries, near, far, labels, mat, gain, bias],
        [by_head, by_head],
        after,
        work(4e9, 1),
    )


def attend_back_body(
    near, far, do_near, do_far, sum_near, sum_far, labels, near_out, far_out,
    qs, ks, vs, grads, dqs, dks, dvs, sums,
):
    head_count = QKV // (3 * HEAD_DIM)
    width = head_count * HEAD_DIM
    half = near.shape[0]
    for start, ref, grad in ((0, near, do_near), (half, far, do_far)):
        split_heads(ref, qs, 0, start, head_count)
        split_heads(ref, ks, width, start, head_count)
        split_heads(ref, vs, 2 * width, start, head_count)
        split_heads(grad, grads, 0, start, head_count)
    sums[:half] = sum_near[...]
    sums[half:] = sum_far[...]
    dks[...] = jnp.zeros_like(dks)
    dvs[...] = jnp.zeros_like(dvs)
    key_labels = labels[0:1, :]
    size = half // 2

    def block(index, carry):
        rows = pl.ds(pl.multiple_of(index * size, size), size)
        allowed = to_columns(labels[:, rows])[:, 0:1] == key_labels
        for head in range(head_count):
            query, grad = qs[head, rows, :], grads[head, rows, :]
            scores = jnp.where(allowed, nt(query, ks[head]), -1e30)
            prob = jnp.exp2(scores * (SCALE * LOG2E) - sums[rows, head : head + 1])
            prob_grad = nt(grad, vs[head])
            delta = jnp.sum(prob * prob_grad, axis=-1, keepdims=True)
            score_grad = (prob * (prob_grad - delta)).astype(BF16)
            dqs[head, rows, :] = nn(score_grad, ks[head]) * SCALE
            dks[head] += tn(query, score_grad)
            dvs[head] += tn(grad, prob.astype(BF16))
        return carry

    lax.fori_loop(0, 4, block, 0)
    for start, out in ((0, near_out), (half, far_out)):
        rows = slice(start, start + half)
        heads = range(head_count)
        out[...] = jnp.concatenate(
            [dqs[head, rows, :].astype(BF16) for head in heads]
            + [(dks[head, :, rows].T * SCALE).astype(BF16) for head in heads]
            + [dvs[head, :, rows].T.astype(BF16) for head in heads],
            axis=1,
        )


def attend_back(near, far, do_near, do_far, sum_near, sum_far, labels, after=()):
    half, width = do_near.shape
    keys = 2 * half
    heads = width // HEAD_DIM
    by_head = pltpu.VMEM((heads, keys, HEAD_DIM), BF16)
    turned = pltpu.VMEM((heads, HEAD_DIM, keys), F32)
    return call(
        "attend_back",
        attend_back_body,
        [(near.shape, BF16)] * 2,
        [near, far, do_near, do_far, sum_near, sum_far, labels],
        [by_head] * 4
        + [pltpu.VMEM((heads, keys, HEAD_DIM), F32), turned, turned, pltpu.VMEM((keys, 128), F32)],
        after,
        work(1.4e10, 1),
    )


def gelu_parts(x):
    spread = 0.5 + 0.5 * lax.erf(x * SQRT_HALF)
    return x * spread, spread


def feed_body(with_back, *refs):
    if with_back:
        one, two, back_one, back_two, mat, gain, bias, f_ref, p_one, p_two, s_ref = refs
    else:
        one, two, mat, gain, bias, f_ref, p_one, p_two = refs
        back_one = back_two = s_ref = None
    size = one.shape[0]
    up, down = mat.at[:, :UNITS], mat.at[:, UNITS:]
    folded = folded_vectors(down[...], gain[...], bias[...])
    for place, (piece, p_ref, back) in enumerate(((one, p_one, back_one), (two, p_two, back_two))):
        rows = slice(place * size, (place + 1) * size)
        pre = nn(piece[...], up[...])
        f_ref[rows, :] = pre
        act, _ = gelu_parts(pre)
        p_ref[:size] = nt((act * gain[...]).astype(BF16), down[...]).astype(BF16)
        columns = [
            jnp.sum(act, axis=-1, keepdims=True),
            jnp.sum(act * act, axis=-1, keepdims=True),
        ]
        p_ref[size : size + TAIL // 2] = encode(to_rows(*columns))
        p_ref[size + TAIL // 2 :] = folded
        if with_back:
            inner = nn(back[...], down[...]) * gain[...]
            columns.append(jnp.sum(inner, axis=-1, keepdims=True))
            columns.append(jnp.sum(inner * act, axis=-1, keepdims=True))
            s_ref[8 * place : 8 * place + 8, :] = to_rows(*columns)


def feed(pieces, backs, mat, gain, bias, after=()):
    size = pieces[0].shape[0]
    outs = [((2 * size, UNITS), F32)] + [((size + TAIL, D), BF16)] * 2
    if backs:
        outs += [((16, size), F32)]
    return call(
        "feed",
        partial(feed_body, bool(backs)),
        outs,
        [*pieces, *backs, mat, gain, bias],
        after=after,
    )


def feed_back_body(first_piece, *refs):
    if first_piece is not None:
        one, two, s_ref, *refs = refs
    else:
        one, two, *refs = refs
        s_ref = None
    f_ref, gain, bias, mat, df_ref, n_ref, p_one, p_two, vec_ref = refs
    up, down = mat.at[:, :UNITS], mat.at[:, UNITS:]
    size = p_one.shape[0]
    gain_grad = jnp.zeros((1, UNITS), F32)
    bias_grad = jnp.zeros((1, UNITS), F32)
    for place, (piece, p_ref) in enumerate(((one, p_one), (two, p_two))):
        rows = slice(place * size, (place + 1) * size)
        upstream = nn(piece[:size], down[...])
        pre = f_ref[rows, :]
        if first_piece is not None:
            start = 8 * (first_piece + place)
            stats = s_ref[start : start + 8, :]
        else:
            stats = decode(piece[size : size + TAIL // 2])
        columns = to_columns(stats)
        mean, scaled, first, second = (columns[:, i : i + 1] for i in range(4))
        act, spread = gelu_parts(pre)
        normal = (act - mean) * scaled
        act_grad = scaled * (upstream * gain[...] - first - normal * second)
        slope = spread + pre * (jnp.exp(-0.5 * pre * pre) * INV_SQRT_2PI)
        pre_grad = (act_grad * slope).astype(BF16)
        df_ref[rows, :] = pre_grad
        n_ref[rows, :] = (normal * gain[...] + bias[...]).astype(BF16)
        p_ref[...] = nt(pre_grad, up[...]).astype(BF16)
        gain_grad += jnp.sum(upstream * normal, axis=0, keepdims=True)
        bias_grad += jnp.sum(upstream, axis=0, keepdims=True)
    vec_ref[...] = vector_rows(gain_grad, bias_grad)


def feed_back(pieces, stats, first_piece, pre, gain, bias, mat, after=()):
    count = pre.shape[0]
    size = count // 2
    return call(
        "feed_back",
        partial(feed_back_body, first_piece if stats else None),
        [((count, UNITS), BF16)] * 2 + [((size, D), BF16)] * 2 + [((8, UNITS), F32)],
        [*pieces, *stats, pre, gain, bias, mat],
        after=after,
    )


def stats_pack_body(near, far, out):
    out[:16] = near[...]
    out[16:] = far[...]


def stats_near_body(stats, got, out):
    for place in range(4):
        other = 8 * (place ^ 1)
        out[8 * place : 8 * place + 8] = stats[8 * place : 8 * place + 8] + got[other : other + 8]


def stats_far_body(stats, got, out):
    for place in range(4):
        other = 8 * (place ^ 2)
        rows = slice(8 * place, 8 * place + 8)
        total = (stats[rows] + got[other : other + 8]) * (1.0 / FF)
        mean, one = total[0:1], total[2:3]
        scaled = lax.rsqrt(total[1:2] - mean * mean + EPS)
        two = scaled * (total[3:4] - mean * one)
        out[rows] = jnp.concatenate([mean, scaled, one, two, total[4:8]], axis=0)


def group_stats(near, far):
    shape = [((32, near.shape[1]), F32)]
    stats = call("stats_pack", stats_pack_body, shape, [near, far])[0]
    stats = call("stats_near", stats_near_body, shape, [stats, core_swap(stats)])[0]
    return call("stats_far", stats_far_body, shape, [stats, x_swap(stats)])[0]


def grads_body(pieces, halves, size, *refs):
    *refs, out = refs
    place = 0
    column = 0
    for left_count, right_count in zip(pieces, halves):
        left = refs[place : place + left_count]
        right = refs[place + left_count : place + left_count + right_count]
        place += left_count + right_count
        width = right[0].shape[1]
        per = left_count // right_count
        total = None
        for index, piece in enumerate(left):
            start = (index % per) * size
            term = tn(piece[:size], right[index // per][start : start + size, :])
            total = term if total is None else total + term
        out[:, column : column + width] = total.astype(BF16)
        column += width


def grads_of(*pairs, after=()):
    pieces = tuple(len(left) for left, _ in pairs)
    halves = tuple(len(right) for _, right in pairs)
    size = pairs[0][1][0].shape[0] // 2
    args = [item for left, right in pairs for item in (*left, *right)]
    width = sum(right[0].shape[1] for _, right in pairs)
    return call(
        "grads",
        partial(grads_body, pieces, halves, size),
        [((D, width), BF16)],
        args,
        after=after,
    )[0]


def inner_back_body(one, two, o_ref, gain, bias, mat, do_ref, u_ref, vec_ref):
    size = o_ref.shape[0] // 2
    gain_grad = jnp.zeros((1, o_ref.shape[1]), F32)
    bias_grad = jnp.zeros((1, o_ref.shape[1]), F32)
    out_mat = mat[:, QKV:]
    for place, piece in enumerate((one, two)):
        rows = slice(place * size, (place + 1) * size)
        upstream = nn(piece[:size], out_mat)
        columns = to_columns(decode(piece[size : size + TAIL // 2]))
        mean, scaled, first, second = (columns[:, i : i + 1] for i in range(4))
        normal = (o_ref[rows, :] - mean) * scaled
        back = scaled * (upstream * gain[...] - first - normal * second)
        do_ref[rows, :] = back.astype(BF16)
        u_ref[rows, :] = (normal * gain[...] + bias[...]).astype(BF16)
        gain_grad += jnp.sum(upstream * normal, axis=0, keepdims=True)
        bias_grad += jnp.sum(upstream, axis=0, keepdims=True)
    vec_ref[...] = vector_rows(gain_grad, bias_grad)


def inner_back(pieces, out, gain, bias, mat, after=()):
    count, width = out.shape
    return call(
        "inner_back",
        inner_back_body,
        [((count, width), BF16)] * 2 + [((8, width), F32)],
        [*pieces, out, gain, bias, mat],
        after=after,
    )


def encode_rows(values):
    return jnp.concatenate(split_three(values), axis=0)


def decode_rows(rows):
    rows = rows.astype(F32)
    count = rows.shape[0] // 3
    return rows[:count] + rows[count : 2 * count] + rows[2 * count :]


def unproject_body(rows, mat, one, two, gain, bias, p_one, p_two, vec_ref):
    size = p_one.shape[0]
    gain_grad = jnp.zeros((1, D), F32)
    bias_grad = jnp.zeros((1, D), F32)
    for place, (piece, p_ref) in enumerate(((one, p_one), (two, p_two))):
        term = nt(rows[place * size : (place + 1) * size], mat[:, :QKV])
        p_ref[...] = term.astype(BF16)
        gain_grad += jnp.sum(term * (piece[...].astype(F32) - bias[...]), axis=0, keepdims=True)
        bias_grad += jnp.sum(term, axis=0, keepdims=True)
    vec_ref[...] = vector_rows(gain_grad / gain[...], bias_grad)


def unproject(rows, mat, pieces, gain, bias, after=()):
    count = rows.shape[0]
    return call(
        "unproject",
        unproject_body,
        [((count // 2, D), BF16)] * 2 + [((8, D), F32)],
        [rows, mat, *pieces, gain, bias],
        after=after,
    )


def vectors_body(*refs):
    *items, out = refs
    out[...] = jnp.zeros_like(out)
    out[0:2, :] = items[0][0:2, :] + items[1][0:2, :]
    for place, item in enumerate(items[2:]):
        first = 2 * place + 2
        out[first : first + 2, : item.shape[1]] = item[0:2, :]


def vectors_of(items):
    return call("vectors", vectors_body, [((16, D), F32)], list(items))[0]


def outer_body(own, got, out):
    out[...] = own[0:8] + got[0:8]


def all_body(own, outer, got, out):
    out[0:8] = outer[...] + got[...]
    out[8:] = own[8:]


def encode_rows(values):
    return jnp.concatenate(split_three(values), axis=0)


def decode_rows(rows):
    rows = rows.astype(F32)
    count = rows.shape[0] // 3
    return rows[:count] + rows[count : 2 * count] + rows[2 * count :]


def branch_of(own, mate, far, feature_count):
    rows = own.shape[0] - TAIL
    half = rows + TAIL // 2
    pieces = (own, mate, far)
    product = sum(piece[:rows].astype(F32) for piece in pieces)
    stats = sum(decode(piece[rows:half]) for piece in pieces) / feature_count
    folded = sum(decode_vectors(piece[half:]) for piece in pieces)
    mean = stats[0:1]
    scaled = lax.rsqrt(stats[1:2] - mean * mean + EPS)
    kept = jnp.concatenate([mean, scaled, jnp.zeros((6, rows), F32)], axis=0)
    columns = to_columns(kept)
    branch = columns[:, 1:2] * (product - columns[:, 0:1] * folded[0:1])
    return branch, folded[1:2], folded[0:1], kept


def after_attend_body(x_ref, own, mate, far, gain, bias, x2_ref, z_ref, h_ref, fold_ref, kept_ref):
    branch, shift, folded, kept = branch_of(own, mate, far, D)
    mid = x_ref[...].astype(F32) + branch + shift
    x2_ref[...] = mid
    z_ref[...] = branch
    normal, _ = split_norm(mid)
    h_ref[...] = (normal * gain[...] + bias[...]).astype(BF16)
    fold_ref[...] = jnp.broadcast_to(folded, fold_ref.shape)
    kept_ref[...] = kept


def after_attend(x, pieces, gain, bias, after=()):
    rows = x.shape[0]
    return call(
        "after_attend",
        after_attend_body,
        [((rows, D), F32), ((rows, D), F32), ((rows, D), BF16), ((8, D), F32), ((8, rows), F32)],
        [x, *pieces, gain, bias],
        after=after,
    )


def mask_column(labels, rows):
    return (to_columns(labels[:, :rows])[:, 0:1] >= 0).astype(F32)


def after_feed_body(x2, own, mate, far, labels, gain, bias, y_ref, z_ref, h_ref, fold_ref, kept_ref):
    branch, shift, folded, kept = branch_of(own, mate, far, FF)
    out = (mask_column(labels, x2.shape[0]) * (x2[...] + branch + shift)).astype(BF16)
    y_ref[...] = out
    z_ref[...] = branch
    normal, _ = split_norm(out.astype(F32))
    h_ref[...] = (normal * gain[...] + bias[...]).astype(BF16)
    fold_ref[...] = jnp.broadcast_to(folded, fold_ref.shape)
    kept_ref[...] = kept


def after_feed(x2, pieces, labels, gain, bias, after=()):
    rows = x2.shape[0]
    return call(
        "after_feed",
        after_feed_body,
        [((rows, D), BF16), ((rows, D), F32), ((rows, D), BF16), ((8, D), F32), ((8, rows), F32)],
        [x2, *pieces, labels, gain, bias],
        after=after,
    )


def finish_feed_body(x2, own, mate, far, labels, y_ref):
    branch, shift, _, _ = branch_of(own, mate, far, FF)
    y_ref[...] = (mask_column(labels, x2.shape[0]) * (x2[...] + branch + shift)).astype(BF16)


def finish_feed(x2, pieces, labels):
    return call("finish_feed", finish_feed_body, [(x2.shape, BF16)], [x2, *pieces, labels])[0]


def payload_of(grad, branch, folded, kept, feature_count):
    sent = grad.astype(BF16)
    wide = sent.astype(F32)
    means = to_rows(
        jnp.sum(wide * folded, axis=-1, keepdims=True),
        jnp.sum(wide * branch, axis=-1, keepdims=True),
    )
    stats = jnp.concatenate([kept[0:2], means[0:2] / feature_count, kept[4:8]], axis=0)
    tail = jnp.concatenate([encode(stats), jnp.zeros((TAIL // 2, D), BF16)], axis=0)
    return jnp.concatenate([sent, tail], axis=0)


def feed_norm_back_body(
    own, mate, far, g_ref, labels, x2, gain, branch, folded, kept, dx_ref, out_ref, vec_ref
):
    upstream = own[...].astype(F32) + mate[...].astype(F32) + far[...].astype(F32)
    back, gain_grad, bias_grad = norm_back(x2[...], gain[...], upstream)
    total = mask_column(labels, x2.shape[0]) * g_ref[...].astype(F32) + back
    dx_ref[...] = total
    out_ref[...] = payload_of(total, branch[...], folded[0:1], kept[...], D)
    vec_ref[...] = vector_rows(gain_grad, bias_grad)


def feed_norm_back(pieces, grad, labels, x2, gain, branch, folded, kept, after=()):
    rows = x2.shape[0]
    return call(
        "feed_norm_back",
        feed_norm_back_body,
        [((rows, D), F32), ((rows + TAIL, D), BF16), ((8, D), F32)],
        [*pieces, grad, labels, x2, gain, branch, folded, kept],
        after=after,
    )


def first_norm_back_body(has_next, *refs):
    own, mate, far, dx2, x_ref, gain, *refs = refs
    upstream = own[...].astype(F32) + mate[...].astype(F32) + far[...].astype(F32)
    back, _, _ = norm_back(x_ref[...].astype(F32), gain[...], upstream)
    total = (dx2[...] + back).astype(BF16)
    if has_next:
        labels, branch, folded, kept, g_ref, out_ref = refs
        masked = mask_column(labels, dx2.shape[0]) * total.astype(F32)
        out_ref[...] = payload_of(masked, branch[...], folded[0:1], kept[...], FF)
    else:
        (g_ref,) = refs
    g_ref[...] = total


def first_norm_back(pieces, dx2, x, gain, following=(), after=()):
    rows = x.shape[0]
    outs = [((rows, D), BF16)]
    if following:
        outs.append(((rows + TAIL, D), BF16))
    return call(
        "first_norm_back",
        partial(first_norm_back_body, bool(following)),
        outs,
        [*pieces, dx2, x, gain, *following],
        after=after,
    )


def in_hbm(x):
    return pltpu.with_memory_space_constraint(x, pltpu.HBM)


def fetch_all(refs, held, sems):
    copies = [
        pltpu.make_async_copy(ref, spot, sems.at[place])
        for place, (ref, spot) in enumerate(zip(refs, held))
    ]
    for copy in copies:
        copy.start()
    for copy in copies:
        copy.wait()


def first_block_body(
    flags, query, key, value, output, down, up, out, down_out, swap_out, *scratch
):
    *held, sems = scratch
    fetch_all((query, key, value, output, down, up), held, sems)
    width = query.shape[1]
    for place, ref in enumerate(held[:3]):
        out[:, place * width : (place + 1) * width] = ref[...]
    out[:, 3 * width :] = held[3][...].T
    down_out[...] = held[4][...]
    lower = jnp.full((1, D), flags[2], jnp.int32) == 0
    swap_out[:, :D] = jnp.where(lower, down_out[...], held[5][...])
    swap_out[:, D:] = out[:, : D // 2]


def first_block(flags, *blocks):
    return pl.pallas_call(
        first_block_body,
        out_shape=tuple(
            jax.ShapeDtypeStruct((blocks[0].shape[0], width), BF16)
            for width in (D, D, 3 * D // 2)
        ),
        in_specs=[SMEM] + [HBM] * 6,
        out_specs=(VMEM,) * 3,
        scratch_shapes=[pltpu.VMEM(block.shape, BF16) for block in blocks]
        + [pltpu.SemaphoreType.DMA((6,))],
        compiler_params=PARAMS,
        name="first_block",
    )(flags, *map(in_hbm, blocks))


def beside_body(one, two, out):
    width = one.shape[1]
    out[:, :width] = one[...]
    out[:, width:] = two[...]


def beside(one, two, after=()):
    rows, width = one.shape
    return call("beside", beside_body, [((rows, 2 * width), BF16)], [one, two], after=after)[0]


def entry_body(flags, inputs, cotangent, out, far_out, own_in, own_grad, sems):
    size = own_in.shape[0]

    def rows_of(micro):
        return pl.ds(pl.multiple_of(micro * size, size), size)

    across, far, own = rows_of(1 - flags[3]), rows_of(flags[2]), rows_of(flags[3])
    copies = [
        pltpu.make_async_copy(source, target, sems.at[place])
        for place, (source, target) in enumerate(
            (
                (inputs.at[across], out.at[:size]),
                (cotangent.at[across], out.at[size:]),
                (inputs.at[far], far_out.at[:size]),
                (cotangent.at[far], far_out.at[size:]),
                (inputs.at[own], own_in),
                (cotangent.at[own], own_grad),
            )
        )
    ]
    for copy in copies:
        copy.start()
    for copy in copies:
        copy.wait()


def entry(flags, inputs, cotangent):
    rows = inputs.shape[0]
    shapes = [rows, rows, rows // 2, rows // 2]
    return pl.pallas_call(
        entry_body,
        out_shape=tuple(jax.ShapeDtypeStruct((count, D), BF16) for count in shapes),
        in_specs=[SMEM, HBM, HBM],
        out_specs=(VMEM,) * 4,
        scratch_shapes=[pltpu.SemaphoreType.DMA((6,))],
        compiler_params=PARAMS,
        name="entry",
    )(flags, in_hbm(inputs), in_hbm(cotangent))


def enter_body(
    flags, own_in, own_grad, got, labels, gain, bias, x_ref, g_ref, top_ref, h_ref
):
    size, width = x_ref.shape
    here = jnp.full((1, width), flags[0], jnp.int32) == 1
    own = jnp.where(here, own_in[...], got[:size])
    grad = jnp.where(here, own_grad[...], got[size:])
    x_ref[...] = own
    g_ref[...] = grad
    top_ref[...] = (mask_column(labels, size) * grad.astype(F32)).astype(BF16)
    normal, _ = split_norm(own.astype(F32))
    h_ref[...] = (normal * gain[...] + bias[...]).astype(BF16)


def enter(flags, own_in, own_grad, got, labels, gain, bias):
    return call(
        "enter",
        enter_body,
        [(own_in.shape, BF16)] * 4,
        [flags, own_in, own_grad, got, labels, gain, bias],
    )


def enter_far_body(got, labels, gain, bias, top_ref, h_ref):
    size = top_ref.shape[0]
    mask = (to_columns(labels[:, 2 * size : 3 * size])[:, 0:1] >= 0).astype(F32)
    top_ref[...] = (mask * got[size:].astype(F32)).astype(BF16)
    normal, _ = split_norm(got[:size].astype(F32))
    h_ref[...] = (normal * gain[...] + bias[...]).astype(BF16)


def enter_far(got, labels, gain, bias):
    rows = got.shape[0] // 2
    return call(
        "enter_far", enter_far_body, [((rows, D), BF16)] * 2, [got, labels, gain, bias]
    )


def pack_body(*refs):
    *items, out = refs
    size = items[0].shape[0]
    for place, item in enumerate(items):
        out[place * size : (place + 1) * size, :] = item[...]


def pack(items):
    rows, width = items[0].shape
    return call("pack", pack_body, [((len(items) * rows, width), BF16)], list(items))[0]


def unpack_body(flags, own, sent, got_own, got_sent, y_ref, g_ref):
    size = y_ref.shape[0] // 2
    width = y_ref.shape[1]
    here = jnp.full((1, width), flags[0], jnp.int32) == 1
    rows = pl.ds(pl.multiple_of(flags[2] * size, size), size)
    first = pl.ds(pl.multiple_of(flags[3] * size, size), size)
    second = pl.ds(pl.multiple_of((1 - flags[3]) * size, size), size)
    last = slice(2 * size, 3 * size)
    y_ref[first, :] = jnp.where(here, own[rows, :], got_own[rows, :])
    y_ref[second, :] = jnp.where(here, sent[rows, :], got_sent[rows, :])
    g_ref[first, :] = jnp.where(here, own[last, :], got_own[last, :])
    g_ref[second, :] = jnp.where(here, sent[last, :], got_sent[last, :])


def unpack(flags, own, sent, got_own, got_sent):
    rows = 2 * own.shape[0] // 3
    return call(
        "unpack",
        unpack_body,
        [((rows, own.shape[1]), BF16)] * 2,
        [flags, own, sent, got_own, got_sent],
    )


def halve_body(with_vectors, flags, block, across, *refs):
    if with_vectors:
        vectors, got, kept, sent, vec_ref = refs
        total = vectors[...] + got[...]
        vec_ref[...] = total
    else:
        kept, sent = refs
    size = kept.shape[0] // 2
    for place, (out, step) in enumerate(((kept, 0), (kept, 2), (sent, 1), (sent, 3))):
        rows = pl.ds(pl.multiple_of((flags[1] ^ step) * size, size), size)
        spot = slice((place % 2) * size, (place % 2 + 1) * size)
        out[spot] = (block[rows, :].astype(F32) + across[rows, :].astype(F32)).astype(BF16)
    if with_vectors:
        sent[2 * size :] = encode_rows(total)


def halve(flags, block, across, vectors=(), after=(), cost=None):
    rows, width = block.shape
    outs = [((rows // 2, width), BF16)] * 2
    if vectors:
        outs = [outs[0], ((rows // 2 + 48, width), BF16), (vectors[0].shape, F32)]
    return call(
        "halve",
        partial(halve_body, bool(vectors)),
        outs,
        [flags, block, across, *vectors],
        after=after,
        cost=cost,
    )


def quarter_body(with_vectors, kept, got, *refs):
    if with_vectors:
        vectors, own, sent, vec_ref = refs
    else:
        own, sent = refs
    size = own.shape[0]
    for place, out in enumerate((own, sent)):
        rows = slice(place * size, (place + 1) * size)
        out[:size] = (kept[rows].astype(F32) + got[rows].astype(F32)).astype(BF16)
    if with_vectors:
        total = vectors[...] + decode_rows(got[2 * size :])
        vec_ref[...] = total
        sent[size:] = encode_rows(total)


def quarter(kept, got, vectors=(), after=()):
    rows, width = kept.shape
    outs = [((rows // 2, width), BF16)] * 2
    if vectors:
        outs = [outs[0], ((rows // 2 + 48, width), BF16), (vectors[0].shape, F32)]
    return call(
        "quarter",
        partial(quarter_body, bool(vectors)),
        outs,
        [kept, got, *vectors],
        after=after,
    )


def last_body(kept, got, vectors, out, vec_ref):
    size = kept.shape[0]
    out[...] = (kept[...].astype(F32) + got[:size].astype(F32)).astype(BF16)
    vec_ref[...] = vectors[...] + decode_rows(got[size:])


def last_of(kept, got, vectors, after=()):
    outs = [(kept.shape, BF16), (vectors.shape, F32)]
    return call("last", last_body, outs, [kept, got, vectors], after=after)


def total_body(*refs):
    *parts, out = refs
    out[...] = sum(part[...].astype(F32) for part in parts).astype(out.dtype)


def total_of(parts, kind=BF16, after=(), cost=None):
    shape = [(parts[0].shape, kind)]
    return call("total", total_body, shape, list(parts), after=after, cost=cost)[0]


def layers_of(flags, lower, lower_got, upper, upper_got):
    width = lower.shape[1]
    here = jnp.full((1, width), flags[0], jnp.int32) == 1
    first = jnp.full((1, width), flags[2], jnp.int32) == 0
    one = jnp.where(here, lower[...], lower_got[...])
    two = jnp.where(here, upper[...], upper_got[...])
    return jnp.where(first, one, two).astype(F32)


def final_first_body(
    flags, lower, lower_got, upper, upper_got, vec, vec_got, q_ref, k_ref, v_ref, o_ref, vec_ref
):
    width = q_ref.shape[1]
    total = layers_of(flags, lower, lower_got, upper, upper_got)
    for place, ref in enumerate((q_ref, k_ref, v_ref)):
        ref[...] = total[:, place * width : (place + 1) * width]
    o_ref[...] = total[:, 3 * width :].T
    here = jnp.full((1, D), flags[0], jnp.int32) == 1
    vec_ref[...] = jnp.where(here, vec[...], vec_got[...])


def final_first(flags, lower, upper, vectors):
    rows, width = lower[0].shape[0], D // LANES
    return call(
        "final_first",
        final_first_body,
        [((rows, width), F32)] * 3 + [((width, rows), F32), ((16, D), F32)],
        [flags, *lower, *upper, *vectors],
    )


def final_second_body(flags, lower, lower_got, upper, upper_got, up_ref, down_ref):
    total = layers_of(flags, lower, lower_got, upper, upper_got)
    up_ref[...] = total[:, :UNITS]
    down_ref[...] = total[:, UNITS:]


def final_second(flags, lower, upper):
    rows = lower[0].shape[0]
    return call(
        "final_second",
        final_second_body,
        [((rows, UNITS), F32)] * 2,
        [flags, *lower, *upper],
    )


def merge_body(flags, one, two, upper, out):
    size, width = one.shape
    first = jnp.full((1, width), flags[2], jnp.int32) == 0
    for place, ref in enumerate((one, two)):
        rows = slice(place * size, (place + 1) * size)
        out[rows] = jnp.where(first, ref[...], upper[rows])


def merge(flags, one, two, upper):
    return call("merge", merge_body, [(upper.shape, BF16)], [flags, one, two, upper])[0]


def choose_body(flags, one, two, out):
    first = jnp.full((1, out.shape[1]), flags[2], jnp.int32) == 0
    out[...] = jnp.where(first, one[...], two[...])


def choose(flags, one, two, after=()):
    return call("choose", choose_body, [(one.shape, one.dtype)], [flags, one, two], after=after)[0]


def join_body(flags, own, got, out):
    half = own.shape[1]
    first = jnp.full((1, half), flags[2], jnp.int32) == 0
    out[:, :half] = jnp.where(first, own[...], got[...])
    out[:, half:] = jnp.where(first, got[...], own[...])


def join(flags, own, got, after=()):
    rows, half = own.shape
    return call(
        "join", join_body, [((rows, 2 * half), BF16)], [flags, own, got], after=after
    )[0]


def hold_body(ref, out):
    out[...] = ref[...]


def hold(x, after):
    return call("hold", hold_body, [(x.shape, x.dtype)], [x], after=after)[0]


def assemble_body(count, flags, *refs):
    beside, across, out = refs[:count], refs[count:-1], refs[-1]
    size = beside[0].shape[0]
    width = out.shape[1]
    near = jnp.full((1, width), flags[0], jnp.int32) == 1
    for step in range(count):
        rows = pl.ds(pl.multiple_of((flags[1] ^ step) * size, size), size)
        out[rows, :] = jnp.where(near, beside[step][...], across[step][...])


def assemble(flags, beside, across, after=()):
    count, (size, width) = len(beside), beside[0].shape
    return call(
        "assemble",
        partial(assemble_body, count),
        [((count * size, width), BF16)],
        [flags, *beside, *across],
        after=after,
    )[0]


def early_block_body(flags, up, got, first, out):
    width = up.shape[1]
    lower = jnp.full((1, width), flags[2], jnp.int32) == 0
    out[:, :width] = jnp.where(lower, up[...], got[:, :width])
    half = first.shape[1] // 2
    lower = jnp.full((1, half), flags[2], jnp.int32) == 0
    out[:, width:] = jnp.where(lower, got[:, width:], first[:, half:])


def early_block(flags, up, got, first, after=()):
    rows, width = up.shape
    return call(
        "early_block",
        early_block_body,
        [((rows, width + first.shape[1] // 2), BF16)],
        [flags, up, got, first],
        after=after,
    )[0]


def late_block_body(flags, got, down, out):
    width = down.shape[1]
    lower = jnp.full((1, width), flags[2], jnp.int32) == 0
    out[...] = jnp.where(lower, got[:, :width], down[...])


def late_block(flags, got, down, after=()):
    return call(
        "late_block", late_block_body, [(down.shape, BF16)], [flags, got, down], after=after
    )[0]


def parts_body(ref, one, two):
    width = one.shape[1]
    one[...] = ref[:, :width]
    two[...] = ref[:, width:]


def parts_of(x, width, after):
    rows, whole = x.shape
    shapes = [((rows, width), x.dtype), ((rows, whole - width), x.dtype)]
    return call("parts", parts_body, shapes, [x], after=after)


def pick_body(flags, beside, across, out):
    near = jnp.full((1, out.shape[1]), flags[0], jnp.int32) == 1
    out[...] = jnp.where(near, beside[...], across[...])


def pick(flags, beside, across, cost=None):
    return call(
        "pick", pick_body, [(beside.shape, BF16)], [flags, beside, across], cost=cost
    )[0]


def on_device(
    inputs,
    cotangent,
    doc_ids,
    norm_gain,
    norm_bias,
    w_query,
    w_key,
    w_value,
    inner_gain,
    inner_bias,
    w_output,
    feed_gain,
    feed_bias,
    w_up,
    middle_gain,
    middle_bias,
    w_down,
):
    core = lax.axis_index("section")
    lane = lax.axis_index("mp")
    lane_x = lane % 2
    lane_y = lane // 2
    count = lax.axis_size("dp")
    slice_len = inputs.shape[0] // MICRO
    rank = 2 * core + lane_x
    crossing = [(s * 4 + r, s * 4 + (r ^ 2)) for s in range(2) for r in range(4) if s == r // 2]
    returning = [(s * 4 + r, s * 4 + (r ^ 2)) for s in range(2) for r in range(4) if s != r // 2]

    def by_core(first, second):
        return jnp.where(core == 0, first, second)

    def placed(array, layer):
        return [
            lax.ppermute(
                array,
                BOTH,
                [(s * 4 + 2 * m + x, layer * 4 + 2 * s + x) for s in range(2) for x in range(2)],
            )
            for m in range(MICRO)
        ]

    label_grid = lax.dynamic_index_in_dim(
        doc_ids.reshape(LANES, MICRO, slice_len), lane_y, 1, keepdims=False
    )
    order = (rank, 2 * (1 - core) + lane_x, rank ^ 1, 2 * (1 - core) + (1 - lane_x))
    labels = jnp.concatenate(
        [lax.dynamic_index_in_dim(label_grid, item, 0, keepdims=False) for item in order]
    )
    labels = jnp.broadcast_to(labels.astype(F32)[None], (8, LANES * slice_len))

    place = lax.axis_index("dp")
    flags = jnp.stack([core == lane_y, place, core, lane_y]).astype(jnp.int32)

    def line_pairs(step):
        return [
            ((r // 2 * count + i) * LANES + r, (r // 2 * count + (i ^ step)) * LANES + r)
            for i in range(count)
            for r in range(LANES)
        ]

    def along_line(block, step):
        return lax.ppermute(block, ("section", "dp", "mp"), line_pairs(step))

    first, down_block, swapped = first_block(
        flags, w_query[0], w_key[0], w_value[0], w_output[0], w_down[0].T, w_up[0]
    )
    up_block = w_up[0]

    def along_dp(block):
        return lax.all_gather(block, "dp", axis=0, tiled=True)

    def fetched(line, hook=()):
        whole = join(flags, line, core_swap(line), after=hook)
        return whole, lax.ppermute(whole, BOTH, crossing)

    outer_own = jnp.concatenate([norm_gain, norm_bias, feed_gain, feed_bias], axis=0)
    outer_other = core_swap(outer_own)
    split_own = jnp.concatenate([inner_gain, inner_bias, middle_gain, middle_bias], axis=1)
    split_far = y_swap(split_own)
    split_kept = jnp.where(lane_y == core, split_own, split_far)
    split_other = core_swap(jnp.where(lane_y == core, split_far, split_own))

    def small_of(outer, split):
        width = D // LANES
        return (
            [outer[i : i + 1] for i in range(4)],
            [
                split[:, :width],
                split[:, width : 2 * width],
                split[:, 2 * width : 2 * width + UNITS],
                split[:, 2 * width + UNITS :],
            ],
        )

    lower_outer, lower_split = small_of(
        by_core(outer_own, outer_other), by_core(split_kept, split_other)
    )
    upper_outer, upper_split = small_of(
        by_core(outer_other, outer_own), by_core(split_other, split_kept)
    )

    def gather_around(own, near_of, far=None, after=()):
        if far is None:
            far = x_swap(own)
        mate = core_swap(own)
        near = near_of([own, mate])
        far = hold(far, after=[near[0], *after])
        return (own, mate, far, core_swap(far)), near

    def attention(x, h, first, outer, split, hooks, far=None):
        pieces, (near,) = gather_around(
            h, lambda rows: [project(*rows, first)], far, after=hooks[2]
        )
        far = project(pieces[2], pieces[3], first)
        half = 2 * slice_len
        o_far, p_far, p_far_mate, sum_far = attend(
            half, far, near, far, labels, first, split[0], split[1]
        )
        sent = pair_sum(p_far, p_far_mate)
        hooks[0](p_far)
        o_near, p_own, p_mate, sum_near = attend(
            0, near, near, far, labels, first, split[0], split[1], after=[sent]
        )
        arrived = hold(x_swap(sent), after=[p_own])
        terms = (p_own, core_swap(p_mate), arrived)
        x2, branch, h2, folded, kept = after_attend(x, terms, outer[2], outer[3], after=hooks[1])
        state = (pieces, near, far, o_near, o_far, sum_near, sum_far, x, x2, branch, folded, kept)
        return x2, h2, state, arrived

    def attention_back(grad, sums, state, first, outer, split, following, hooks):
        pieces, near, far, o_near, o_far, sum_near, sum_far, x, x2, branch, folded, kept = state
        dx2, sent, feed_vec = feed_norm_back(
            sums, grad, labels, x2, outer[2], branch, folded, kept, after=hooks[0]
        )
        block = hooks[3](sent)
        backs, (do_near, u_near, vec_near) = gather_around(
            sent, lambda rows: inner_back(rows, o_near, split[0], split[1], first), after=block
        )
        do_far, u_far, vec_far = inner_back(backs[2:], o_far, split[0], split[1], first)
        dq_near, dq_far = attend_back(
            near, far, do_near, do_far, sum_near, sum_far, labels, after=hooks[1]
        )
        norm = (outer[0], outer[1])
        p_far, p_far_mate, norm_far = unproject(
            dq_far, first, pieces[2:], *norm, after=hooks[4](dq_far)
        )
        sent = pair_sum(p_far, p_far_mate)
        p_own, p_mate, norm_near = unproject(
            dq_near, first, pieces[:2], *norm, after=[sent, *hooks[5]()]
        )
        mat_grad = grads_of(
            (pieces, (dq_near, dq_far)), (backs, (u_near, u_far)), after=[sent]
        )
        terms = (p_own, core_swap(p_mate), hold(x_swap(sent), after=[p_own, mat_grad]))
        result = first_norm_back(
            terms, dx2, x, outer[0], following, after=hooks[2](mat_grad)
        )
        return result, vec_near + vec_far, feed_vec, (norm_near, norm_far)

    def reduce_across(block):
        across = lax.ppermute(block, BOTH, returning)
        if count != 4:
            total = total_of([block, across])
            return [lax.psum_scatter(total, "dp", scatter_dimension=0, tiled=True)]
        return block, across

    def reduce_near(pair, after=(), cost=None):
        if count != 4:
            return pair
        kept, sent = halve(flags, *pair, after=after, cost=cost)
        return kept, along_line(sent, 1)

    def reduce_far(pair, after=()):
        if count != 4:
            return pair
        kept, sent = quarter(*pair, after=after)
        return kept, along_line(sent, 2)

    def reduce_end(pair, after=(), cost=None):
        total = total_of(pair, after=after, cost=cost) if count == 4 else pair[0]
        return total, core_swap(total)

    sent, far_sent, own_in, own_grad = entry(flags, inputs, cotangent)
    got = lax.ppermute(sent, BOTH, crossing)
    far_got = lax.ppermute(
        far_sent,
        BOTH,
        [
            (s * LANES + r, s * LANES + (r ^ 1) if s == r // 2 else (r // 2) * LANES + (r ^ 3))
            for s in range(2)
            for r in range(LANES)
        ],
    )
    lower_in, upstream, masked, h = enter(
        flags, own_in, own_grad, got, labels, lower_outer[0], lower_outer[1]
    )
    masked_far, far = enter_far(far_got, labels, lower_outer[0], lower_outer[1])
    top = (masked, core_swap(masked), masked_far, core_swap(masked_far))
    moved = choose(flags, first, core_swap(first))
    if count == 4:
        pieces = [moved] + [along_line(moved, step) for step in range(1, count)]
        lower_first = assemble(
            flags, pieces, [lax.ppermute(piece, BOTH, crossing) for piece in pieces], after=[far]
        )
    else:
        pieces = [along_dp(moved)]
        lower_first = pick(flags, pieces[0], lax.ppermute(pieces[0], BOTH, crossing))
    got = core_swap(swapped)
    early_line = along_dp(early_block(flags, up_block, got, first, after=pieces[-1:]))
    late_line = along_dp(late_block(flags, got, down_block))
    coming = {}

    def early_matrices(last):
        coming["second"], coming["first"] = parts_of(early_line, UNITS, [last])

    x2, h2, lower_state, arrived = attention(
        lower_in, h, lower_first, lower_outer, lower_split, (early_matrices, (), ()), far
    )
    lower_second_whole, lower_second_across = fetched(coming["second"])
    lower_second = pick(flags, lower_second_whole, lower_second_across)
    upper_first_whole, upper_first_across = fetched(coming["first"], [h2])
    upper_first = pick(flags, upper_first_whole, upper_first_across)
    lower_pieces, (f_near, p_own, p_mate) = gather_around(
        h2, lambda rows: feed(rows, (), lower_second, *lower_split[2:])
    )
    f_far, p_far, p_far_mate = feed(lower_pieces[2:], (), lower_second, *lower_split[2:])
    lower_pre = (f_near, f_far)
    sent = pair_sum(p_far, p_far_mate)
    upper_second_whole, upper_second_across = fetched(hold(late_line, after=[sent]))
    upper_second = pick(flags, upper_second_whole, upper_second_across, work(1e10, 1))
    arrived = hold(x_swap(sent), after=[upper_second_whole])
    terms = (p_own, core_swap(p_mate), arrived)
    lower_out, lower_branch, h, lower_folded, lower_kept = after_feed(
        x2, terms, labels, upper_outer[0], upper_outer[1]
    )
    x2, h2, upper_state, _ = attention(
        lower_out,
        h,
        upper_first,
        upper_outer,
        upper_split,
        (lambda last: None, (), [upper_second_whole]),
    )
    upper_pieces, (f_near, p_own, p_mate, near_stats) = gather_around(
        h2, lambda rows: feed(rows, top[:2], upper_second, *upper_split[2:])
    )
    f_far, p_far, p_far_mate, far_stats = feed(
        upper_pieces[2:], top[2:], upper_second, *upper_split[2:]
    )
    upper_pre = (f_near, f_far)

    stats = group_stats(near_stats, far_stats)
    df_far, n_far, q_far, q_far_mate, vec_far = feed_back(
        top[2:], [stats], 2, upper_pre[1], *upper_split[2:], upper_second
    )
    sent = pair_sum(q_far, q_far_mate)
    df_near, n_near, q_own, q_mate, vec_near = feed_back(
        top[:2], [stats], 0, upper_pre[0], *upper_split[2:], upper_second, after=[sent]
    )
    upper_middle = vec_near + vec_far
    sums = (q_own, core_swap(q_mate), hold(x_swap(sent), after=[q_own]))
    ended = pair_sum(p_far, p_far_mate)
    ended_far = []

    def ended_hook(last):
        ended_far.append(hold(x_swap(ended), after=[last]))
        return ended_far

    following = (labels, lower_branch, lower_folded, lower_kept)
    pairs = {}

    def upper_second_grads(after):
        block = grads_of(
            (upper_pieces, (df_near, df_far)), (top, (n_near, n_far)), after=[after]
        )
        pairs["second"] = reduce_near(reduce_across(block), cost=work(9e9, 1))
        return [block]

    def upper_hook(item):
        pairs["upper"] = reduce_across(item)
        return [item]

    (upper_grad, sent), upper_inner, upper_feed, upper_norm = attention_back(
        upstream,
        sums,
        upper_state,
        upper_first,
        upper_outer,
        upper_split,
        following,
        ((), [ended], upper_hook, upper_second_grads, ended_hook, lambda: ()),
    )

    upper_out = finish_feed(x2, (p_own, core_swap(p_mate), ended_far[0]), labels)
    own = pack([lower_out, upper_out, upper_grad])
    swapped = lax.ppermute(own, BOTH, returning)
    upper_second_pair = reduce_far(pairs["second"], [own])
    upper_first_pair = reduce_near(pairs["upper"])
    backs, (df_near, n_near, q_own, q_mate, vec_near) = gather_around(
        sent,
        lambda rows: feed_back(
            rows, (), 0, lower_pre[0], *lower_split[2:], lower_second, after=[own]
        ),
        after=upper_first_pair[:1],
    )
    df_far, n_far, q_far, q_far_mate, vec_far = feed_back(
        backs[2:],
        (),
        2,
        lower_pre[1],
        *lower_split[2:],
        lower_second,
        after=[upper_second_pair[0]],
    )
    lower_middle = vec_near + vec_far
    sent = pair_sum(q_far, q_far_mate)
    sums = (q_own, core_swap(q_mate), x_swap(sent))

    def lower_second_grads(after):
        block = grads_of(
            (lower_pieces, (df_near, df_far)), (backs, (n_near, n_far)), after=[after]
        )
        pairs["second"] = reduce_across(block)
        return [block]

    upper_first_pair = reduce_far(upper_first_pair, after=[q_far])

    layer_outputs, upper_held = unpack(
        flags, own, swapped, core_swap(own), core_swap(swapped)
    )

    def lower_hook(item):
        pairs["lower"] = reduce_across(item)
        pairs["second"] = reduce_near(pairs["second"], after=[item])
        return [item]

    def upper_ended(last):
        pairs["ended"] = reduce_end(upper_second_pair, after=[last])
        pairs["first"] = reduce_end(upper_first_pair, after=[last])
        return [pairs["ended"][0], pairs["first"][0]]

    (lower_grad,), lower_inner, lower_feed, lower_norm = attention_back(
        upper_grad,
        sums,
        lower_state,
        lower_first,
        lower_outer,
        lower_split,
        (),
        (
            [upper_first_pair[0]],
            [layer_outputs],
            lower_hook,
            lower_second_grads,
            upper_ended,
            lambda: (),
        ),
    )
    vectors = vectors_of(
        [*lower_norm, lower_feed, upper_norm[0] + upper_norm[1], upper_feed]
        + [lower_middle, upper_middle, lower_inner, upper_inner]
    )
    outer = call("outer", outer_body, [((8, D), F32)], [vectors, core_swap(vectors)])[0]
    vectors = call("all", all_body, [((16, D), F32)], [vectors, outer, x_swap(outer)])[0]
    lower_held = placed(lower_grad, 0)
    input_grads = merge(flags, *lower_held, upper_held)
    if count == 4:
        first_kept, sent, vectors = halve(
            flags,
            *pairs["lower"],
            (vectors, y_swap(vectors)),
            after=[pairs["first"][0], lower_grad],
        )
        got = along_line(sent, 1)
        lower_second_sum = reduce_end(reduce_far(pairs["second"], after=[first_kept]))
        grad_up, grad_down = final_second(flags, lower_second_sum, pairs["ended"])
        kept, sent, vectors = quarter(first_kept, got, [vectors])
        ended, vectors = last_of(
            kept, along_line(sent, 2), vectors, after=[input_grads, grad_up]
        )
    else:
        vectors = lax.psum(vectors + y_swap(vectors), "dp")
        ended = pairs["lower"][0]
        lower_second_sum = reduce_end(pairs["second"])
        grad_up, grad_down = final_second(flags, lower_second_sum, pairs["ended"])
    grad_query, grad_key, grad_value, grad_output, vectors = final_first(
        flags, (ended, core_swap(ended)), pairs["first"], (vectors, core_swap(vectors))
    )

    def part(rows, start, size):
        rows = lax.dynamic_slice(rows, (core * rows.shape[0] // 2, start), (rows.shape[0] // 2, size))
        return [rows[i : i + 1] for i in range(rows.shape[0])]

    width = D // LANES
    size = D // count // LANES
    outer = part(vectors[:8], (place * LANES + lane) * size, size)
    middle = part(vectors[8:12], place * (UNITS // count), UNITS // count)
    inner = part(vectors[12:], place * (width // count), width // count)
    return (
        layer_outputs[None],
        input_grads[None],
        outer[0],
        outer[1],
        grad_query[None],
        grad_key[None],
        grad_value[None],
        inner[0],
        inner[1],
        grad_output[None],
        outer[2],
        outer[3],
        grad_up[None],
        middle[0],
        middle[1],
        grad_down.T[None],
    )


def solution(mesh):
    placed = (
        P(("dp", "mp"), None),
        P(("dp", "mp"), None),
        P("dp"),
        P("section", None),
        P("section", None),
        P("section", "dp", "mp"),
        P("section", "dp", "mp"),
        P("section", "dp", "mp"),
        P("section", "mp"),
        P("section", "mp"),
        P("section", "mp", "dp"),
        P("section", None),
        P("section", None),
        P("section", "dp", "mp"),
        P("section", "mp"),
        P("section", "mp"),
        P("section", "mp", "dp"),
    )
    return jax.shard_map(
        on_device,
        mesh=mesh,
        in_specs=placed,
        out_specs=(
            P("section", ("dp", "mp"), None),
            P("section", ("dp", "mp"), None),
            P("section", ("dp", "mp")),
            P("section", ("dp", "mp")),
            P("section", "dp", "mp"),
            P("section", "dp", "mp"),
            P("section", "dp", "mp"),
            P("section", ("mp", "dp")),
            P("section", ("mp", "dp")),
            P("section", "mp", "dp"),
            P("section", ("dp", "mp")),
            P("section", ("dp", "mp")),
            P("section", "dp", "mp"),
            P("section", ("mp", "dp")),
            P("section", ("mp", "dp")),
            P("section", "mp", "dp"),
        ),
        check_vma=False,
    )
```

profile of v0, /device:TPU:0, one launch (start us, length us, event | category | flops | bytes accessed | tf_op | source)
XLA Modules:
  0.0 409.2 jit_solution(583588399968285025)
XLA Ops:
  7.3 2.1 first_block.1
  11.7 6.9 %collective-permute-start.6 = (bf16[192,768]{1,0:T(8,128)(2,1)S(1)}, bf16[192,768]{1,0:T(8,128)(2,1)S(1)}, u32[]{:S(2)}, u32[]{:S(2)}) collective-permute-start(bf16[192,768]{1,0:T(8,128)(2,1)S(1)} %choose.1.refs_1_), channel_id=1, source_target_pairs={{0,12},{1,13},{18,30},{19,31},{4,8},{5,9},{22,26},{23,27},{8,4},{9... | collective-permute-start | bytes 884744 | tf_op jit(solution)/shard_map/ppermute | solution.py:1199
  18.6 4.8 %collective-permute-done.6.refs_4_ = bf16[192,768]{1,0:T(8,128)(2,1)S(1)} collective-permute-done((bf16[192,768]{1,0:T(8,128)(2,1)S(1)}, bf16[192,768]{1,0:T(8,128)(2,1)S(1)}, u32[]{:S(2)}, u32[]{:S(2)}) %collective-permute-start.6) | collective-permute-done | bytes 294944 | tf_op jit(solution)/shard_map/ppermute | solution.py:1199
  25.7 3.4 entry.1
  30.5 1.8 collective-permute-start.11
  32.5 4.7 %collective-permute-start.4 = (bf16[192,768]{1,0:T(8,128)(2,1)S(1)}, bf16[192,768]{1,0:T(8,128)(2,1)S(1)}, u32[]{:S(2)}, u32[]{:S(2)}) collective-permute-start(bf16[192,768]{1,0:T(8,128)(2,1)S(1)} %choose.1.refs_1_), channel_id=1, source_target_pairs={{0,4},{1,5},{18,22},{19,23},{4,0},{5,1},{22,18},{23,19},{8,12},{9,... | collective-permute-start | bytes 884744 | tf_op jit(solution)/shard_map/ppermute | solution.py:1199
  37.3 3.2 collective-permute-start.5
  42.5 5.2 %collective-permute-done.refs_3_ = bf16[512,768]{1,0:T(8,128)(2,1)S(1)} collective-permute-done((bf16[512,768]{1,0:T(8,128)(2,1)}, bf16[512,768]{1,0:T(8,128)(2,1)S(1)}, u32[]{:S(2)}, u32[]{:S(2)}) %collective-permute-start) | collective-permute-done | bytes 786464 | tf_op jit(solution)/shard_map/ppermute | solution.py:1321
  47.7 2.5 collective-permute-start.13
  53.3 2.9 collective-permute-start.10
  59.2 4.2 %collective-permute-done.5.refs_3_ = bf16[192,768]{1,0:T(8,128)(2,1)S(1)} collective-permute-done((bf16[192,768]{1,0:T(8,128)(2,1)S(1)}, bf16[192,768]{1,0:T(8,128)(2,1)S(1)}, u32[]{:S(2)}, u32[]{:S(2)}) %collective-permute-start.5) | collective-permute-done | bytes 294944 | tf_op jit(solution)/shard_map/ppermute | solution.py:1199
  66.6 2.3 collective-permute-done.9.refs_7_
  73.2 5.0 %attend.4 = (f32[512,192]{1,0:T(8,128)S(1)}, bf16[272,768]{1,0:T(8,128)(2,1)S(1)}, bf16[272,768]{1,0:T(8,128)(2,1)}, f32[512,128]{1,0:T(8,128)S(1)}) custom-call(bf16[512,576]{1,0:T(8,128)(2,1)S(1)} %project.5.refs_0_.refs_2_.refs_1_, bf16[512,576]{1,0:T(8,128)(2,1)S(1)} %project.4.refs_1_.refs_0_, bf16[512,576]{1,0:T(8,128)(2,1)S(1)} %project.5.refs_0_.refs_2_.refs_1_, ...), custom_call_target="tpu_custom_call" | custom-call | flops 4000000000 | bytes 1 | tf_op jit(solution)/shard_map/attend/pallas_call | solution.py:41
  83.2 2.7 collective-permute-done.20.refs_2_
  86.7 6.0 %collective-permute-start.21 = (bf16[768,1536]{1,0:T(8,128)(2,1)S(1)}, bf16[768,1536]{1,0:T(8,128)(2,1)}, u32[]{:S(2)}, u32[]{:S(2)}) collective-permute-start(bf16[768,1536]{1,0:T(8,128)(2,1)S(1)} %join.3.refs_1_), channel_id=1, source_target_pairs={{0,2},{1,3},{18,16},{19,17},{4,6},{5,7},{22,20},{23,21},{8,10},{9,... | collective-permute-start | bytes 7077896 | tf_op jit(solution)/shard_map/ppermute | solution.py:1211
  99.6 4.2 %attend.5 = (f32[512,192]{1,0:T(8,128)S(1)}, bf16[272,768]{1,0:T(8,128)(2,1)S(1)}, bf16[272,768]{1,0:T(8,128)(2,1)S(1)}, f32[512,128]{1,0:T(8,128)S(1)}) custom-call(bf16[512,576]{1,0:T(8,128)(2,1)S(1)} %copy-done.24, bf16[512,576]{1,0:T(8,128)(2,1)S(1)} %copy-done.24, bf16[512,576]{1,0:T(8,128)(2,1)S(1)} %copy-done.52, f32[8,1024]{1,0:T(8,128)S(1)} %copy-done.27, ...), custom_call_target="tpu_custom_call" | custom-call | flops 4000000000 | bytes 1 | tf_op jit(solution)/shard_map/attend/pallas_call | solution.py:41
  105.4 3.3 collective-permute-done.17.refs_0_
  112.9 4.5 %collective-permute-done.21.refs_2_ = bf16[768,1536]{1,0:T(8,128)(2,1)} collective-permute-done((bf16[768,1536]{1,0:T(8,128)(2,1)S(1)}, bf16[768,1536]{1,0:T(8,128)(2,1)}, u32[]{:S(2)}, u32[]{:S(2)}) %collective-permute-start.21) | collective-permute-done | bytes 2359328 | tf_op jit(solution)/shard_map/ppermute | solution.py:1211
  117.4 1.9 pick.3.refs_2_.refs_5_
  119.4 1.9 feed.4
  122.0 2.0 collective-permute-done.23.refs_0_
  125.9 1.9 feed.5
  136.4 3.8 collective-permute-start.30
  141.2 8.2 %collective-permute-done.26.refs_0_ = bf16[272,768]{1,0:T(8,128)(2,1)S(1)} collective-permute-done((bf16[272,768]{1,0:T(8,128)(2,1)S(1)}, bf16[272,768]{1,0:T(8,128)(2,1)S(1)}, u32[]{:S(2)}, u32[]{:S(2)}) %collective-permute-start.26) | collective-permute-done | bytes 417824 | tf_op jit(solution)/shard_map/ppermute | solution.py:152
  150.8 4.6 %collective-permute-start.38 = (bf16[768,1536]{1,0:T(8,128)(2,1)S(1)}, bf16[768,1536]{1,0:T(8,128)(2,1)S(1)}, u32[]{:S(2)}, u32[]{:S(2)}) collective-permute-start(bf16[768,1536]{1,0:T(8,128)(2,1)S(1)} %join.4.refs_1_.refs_2_), channel_id=1, source_target_pairs={{0,2},{1,3},{18,16},{19,17},{4,6},{5,7},{22,20},{23,21},{8,10},{9,... | collective-permute-start | bytes 7077896 | tf_op jit(solution)/shard_map/ppermute | solution.py:1211
  156.9 5.1 %collective-permute-done.31.refs_0_ = bf16[256,768]{1,0:T(8,128)(2,1)S(1)} collective-permute-done((bf16[256,768]{1,0:T(8,128)(2,1)S(1)}, bf16[256,768]{1,0:T(8,128)(2,1)S(1)}, u32[]{:S(2)}, u32[]{:S(2)}) %collective-permute-start.31) | collective-permute-done | bytes 393248 | tf_op jit(solution)/shard_map/ppermute | solution.py:152
  164.5 4.2 %attend.6 = (f32[512,192]{1,0:T(8,128)S(1)}, bf16[272,768]{1,0:T(8,128)(2,1)S(1)}, bf16[272,768]{1,0:T(8,128)(2,1)S(1)}, f32[512,128]{1,0:T(8,128)S(1)}) custom-call(bf16[512,576]{1,0:T(8,128)(2,1)S(1)} %project.7.refs_0_.refs_2_.refs_1_, bf16[512,576]{1,0:T(8,128)(2,1)S(1)} %project.6.refs_1_.refs_0_, bf16[512,576]{1,0:T(8,128)(2,1)S(1)} %project.7.refs_0_.refs_2_.refs_1_, ...), custom_call_target="tpu_custom_call" | custom-call | flops 4000000000 | bytes 1 | tf_op jit(solution)/shard_map/attend/pallas_call | solution.py:41
  171.1 4.2 %attend.7 = (f32[512,192]{1,0:T(8,128)S(1)}, bf16[272,768]{1,0:T(8,128)(2,1)S(1)}, bf16[272,768]{1,0:T(8,128)(2,1)S(1)}, f32[512,128]{1,0:T(8,128)S(1)}) custom-call(bf16[512,576]{1,0:T(8,128)(2,1)S(1)} %project.6.refs_1_.refs_0_, bf16[512,576]{1,0:T(8,128)(2,1)S(1)} %project.6.refs_1_.refs_0_, bf16[512,576]{1,0:T(8,128)(2,1)S(1)} %project.7.refs_0_.refs_2_.refs_1_, ...), custom_call_target="tpu_custom_call" | custom-call | flops 4000000000 | bytes 1 | tf_op jit(solution)/shard_map/attend/pallas_call | solution.py:41
  176.0 6.5 %collective-permute-done.35.refs_0_ = bf16[272,768]{1,0:T(8,128)(2,1)S(1)} collective-permute-done((bf16[272,768]{1,0:T(8,128)(2,1)S(1)}, bf16[272,768]{1,0:T(8,128)(2,1)S(1)}, u32[]{:S(2)}, u32[]{:S(2)}) %collective-permute-start.35) | collective-permute-done | bytes 417824 | tf_op jit(solution)/shard_map/ppermute | solution.py:152
  185.1 3.0 feed.6
  188.1 6.8 %collective-permute-done.40.refs_0_ = bf16[256,768]{1,0:T(8,128)(2,1)S(1)} collective-permute-done((bf16[256,768]{1,0:T(8,128)(2,1)S(1)}, bf16[256,768]{1,0:T(8,128)(2,1)S(1)}, u32[]{:S(2)}, u32[]{:S(2)}) %collective-permute-start.40) | collective-permute-done | bytes 393248 | tf_op jit(solution)/shard_map/ppermute | solution.py:152
  196.7 2.6 feed.7
  200.8 3.6 collective-permute-done.46.refs_1_
  204.5 2.3 feed_back.4
  209.1 2.3 feed_back.5
  211.5 8.4 %collective-permute-done.49.refs_0_ = bf16[256,768]{1,0:T(8,128)(2,1)S(1)} collective-permute-done((bf16[256,768]{1,0:T(8,128)(2,1)S(1)}, bf16[256,768]{1,0:T(8,128)(2,1)S(1)}, u32[]{:S(2)}, u32[]{:S(2)}) %collective-permute-start.49) | collective-permute-done | bytes 393248 | tf_op jit(solution)/shard_map/ppermute | solution.py:152
  221.5 2.9 grads.4.refs_2_.refs_1_
  225.7 3.1 collective-permute-start.43
  229.5 3.7 collective-permute-done.51.refs_0_
  235.7 13.1 %attend_back.2 = (bf16[512,576]{1,0:T(8,128)(2,1)S(1)}, bf16[512,576]{1,0:T(8,128)(2,1)S(1)}) custom-call(bf16[512,576]{1,0:T(8,128)(2,1)S(1)} %project.6.refs_1_.refs_0_, bf16[512,576]{1,0:T(8,128)(2,1)S(1)} %project.7.refs_0_.refs_2_.refs_1_, bf16[512,192]{1,0:T(8,128)(2,1)S(1)} %get-tuple-element.212.refs_1_.refs_2_, ...), custom_call_target="tpu_custom_call" | custom-call | flops 14000000000 | bytes 1 | tf_op jit(solution)/shard_map/attend_back/pallas_call | solution.py:41
  253.1 1.9 grads.5.refs_2_.refs_10_.refs_1_
  257.5 4.1 collective-permute-start.65
  266.7 2.4 feed_back.6
  269.0 4.1 collective-permute-done.62.refs_2_
  273.9 2.1 collective-permute-done.61.refs_0_
  277.9 2.4 feed_back.7
  280.5 2.9 collective-permute-start.68
  285.7 6.5 %collective-permute-done.68.refs_1_ = bf16[384,768]{1,0:T(8,128)(2,1)S(1)} collective-permute-done((bf16[384,768]{1,0:T(8,128)(2,1)S(1)}, bf16[384,768]{1,0:T(8,128)(2,1)S(1)}, u32[]{:S(2)}, u32[]{:S(2)}) %collective-permute-start.68) | collective-permute-done | bytes 589856 | tf_op jit(solution)/shard_map/ppermute | solution.py:1199
  292.4 2.8 collective-permute-done.67.refs_2_
  298.0 2.8 grads.6.refs_2_.refs_1_
  303.2 5.3 %collective-permute-done.70.refs_0_ = bf16[272,768]{1,0:T(8,128)(2,1)S(1)} collective-permute-done((bf16[272,768]{1,0:T(8,128)(2,1)S(1)}, bf16[272,768]{1,0:T(8,128)(2,1)S(1)}, u32[]{:S(2)}, u32[]{:S(2)}) %collective-permute-start.70) | collective-permute-done | bytes 417824 | tf_op jit(solution)/shard_map/ppermute | solution.py:152
  308.6 4.1 collective-permute-start.72
  312.7 2.8 collective-permute-start.73
  318.8 13.1 %attend_back.3 = (bf16[512,576]{1,0:T(8,128)(2,1)S(1)}, bf16[512,576]{1,0:T(8,128)(2,1)S(1)}) custom-call(bf16[512,576]{1,0:T(8,128)(2,1)S(1)} %copy-done.25, bf16[512,576]{1,0:T(8,128)(2,1)S(1)} %copy-done.53, bf16[512,192]{1,0:T(8,128)(2,1)S(1)} %get-tuple-element.253.refs_1_.refs_2_, bf16[512,192]{1,0:T(8,128)(2,1)S(1)} %get-tuple-element.258.refs_3_, ...), custom_call_target="tpu_custom_call" | custom-call | flops 14000000000 | bytes 1 | tf_op jit(solution)/shard_map/attend_back/pallas_call | solution.py:41
  332.0 1.9 collective-permute-done.73.refs_1_
  336.8 1.9 grads.7.refs_2_.refs_6_.refs_1_.refs_3_
  341.1 2.2 collective-permute-start.86
  348.1 7.3 %collective-permute-done.81.refs_2_ = f32[8,768]{1,0:T(8,128)S(1)} collective-permute-done((f32[8,768]{1,0:T(8,128)S(1)}, f32[8,768]{1,0:T(8,128)S(1)}, u32[]{:S(2)}, u32[]{:S(2)}) %collective-permute-start.81) | collective-permute-done | bytes 24608 | tf_op jit(solution)/shard_map/ppermute | solution.py:152
  360.6 3.7 collective-permute-start.87
  364.4 3.1 collective-permute-start.83
  367.6 12.2 %collective-permute-done.87.refs_1_ = bf16[192,1536]{1,0:T(8,128)(2,1)S(1)} collective-permute-done((bf16[192,1536]{1,0:T(8,128)(2,1)S(1)}, bf16[192,1536]{1,0:T(8,128)(2,1)S(1)}, u32[]{:S(2)}, u32[]{:S(2)}) %collective-permute-start.87) | collective-permute-done | bytes 589856 | tf_op jit(solution)/shard_map/ppermute | solution.py:1199
  383.2 1.9 collective-permute-start.84
  386.4 3.9 collective-permute-done.78.refs_2_
  393.5 2.9 collective-permute-done.84.refs_1_
  (454 shorter events, 128.6 us)
Async XLA Ops:
  7.2 73.3 %all-gather.3.cloned.1.call-start = ((), (), s32[]{:S(2)}) async-start(), calls=%async_computation | async-start | bytes 2211840 | tf_op jit(solution)/shard_map/all_gather | solution.py:1207
  9.9 8.7 %collective-permute-start.19 = (bf16[192,1152]{1,0:T(8,128)(2,1)S(1)}, bf16[192,1152]{1,0:T(8,128)(2,1)S(1)}, u32[]{:S(2)}, u32[]{:S(2)}) collective-permute-start(bf16[192,1152]{1,0:T(8,128)(2,1)S(1)} %get-tuple-element.175), channel_id=1, source_target_pairs={{0,16},{16,0},{1,17},{17,1},{2,18},{18,2},{3,19},{19,3},{4,20},{20... | collective-permute-start | bytes 1327112 | tf_op jit(solution)/shard_map/ppermute | solution.py:148
  11.7 11.7 %collective-permute-start.6 = (bf16[192,768]{1,0:T(8,128)(2,1)S(1)}, bf16[192,768]{1,0:T(8,128)(2,1)S(1)}, u32[]{:S(2)}, u32[]{:S(2)}) collective-permute-start(bf16[192,768]{1,0:T(8,128)(2,1)S(1)} %choose.1.refs_1_), channel_id=1, source_target_pairs={{0,12},{1,13},{18,30},{19,31},{4,8},{5,9},{22,26},{23,27},{8,4},{9... | collective-permute-start | bytes 884744 | tf_op jit(solution)/shard_map/ppermute | solution.py:1199
  25.6 106.1 %all-gather.5.cloned.1.call-start = ((), (), s32[]{:S(2)}) async-start(), calls=%async_computation.1 | async-start | bytes 1474560 | tf_op jit(solution)/shard_map/all_gather | solution.py:1207
  29.0 18.6 %collective-permute-start = (bf16[512,768]{1,0:T(8,128)(2,1)}, bf16[512,768]{1,0:T(8,128)(2,1)S(1)}, u32[]{:S(2)}, u32[]{:S(2)}) collective-permute-start(bf16[512,768]{1,0:T(8,128)(2,1)} %get-tuple-element.163), channel_id=1, source_target_pairs={{0,2},{1,3},{18,16},{19,17},{4,6},{5,7},{22,20},{23,21},{8,10},{9,... | collective-permute-start | bytes 2359304 | tf_op jit(solution)/shard_map/ppermute | solution.py:1321
  30.4 10.1 %collective-permute-start.1 = (f32[4,768]{1,0:T(4,128)S(1)}, f32[4,768]{1,0:T(4,128)S(1)}, u32[]{:S(2)}, u32[]{:S(2)}) collective-permute-start(f32[4,768]{1,0:T(4,128)S(1)} %pad_maximum_fusion), channel_id=1, source_target_pairs={{0,16},{16,0},{1,17},{17,1},{2,18},{18,2},{3,19},{19,3},{4,20},{20... | collective-permute-start | bytes 36872 | tf_op jit(solution)/shard_map/ppermute | solution.py:148
  30.5 34.3 %collective-permute-start.11 = (bf16[512,768]{1,0:T(8,128)(2,1)}, bf16[512,768]{1,0:T(8,128)(2,1)S(1)}, u32[]{:S(2)}, u32[]{:S(2)}) collective-permute-start(bf16[512,768]{1,0:T(8,128)(2,1)} %get-tuple-element.167), channel_id=1, source_target_pairs={{0,1},{1,0},{2,17},{3,16},{16,3},{17,2},{18,19},{19,18},{4,5},{5,4... | collective-permute-start | bytes 2359304 | tf_op jit(solution)/shard_map/ppermute | solution.py:1322
  32.5 25.4 %collective-permute-start.4 = (bf16[192,768]{1,0:T(8,128)(2,1)S(1)}, bf16[192,768]{1,0:T(8,128)(2,1)S(1)}, u32[]{:S(2)}, u32[]{:S(2)}) collective-permute-start(bf16[192,768]{1,0:T(8,128)(2,1)S(1)} %choose.1.refs_1_), channel_id=1, source_target_pairs={{0,4},{1,5},{18,22},{19,23},{4,0},{5,1},{22,18},{23,19},{8,12},{9,... | collective-permute-start | bytes 884744 | tf_op jit(solution)/shard_map/ppermute | solution.py:1199
  37.3 26.2 %collective-permute-start.5 = (bf16[192,768]{1,0:T(8,128)(2,1)S(1)}, bf16[192,768]{1,0:T(8,128)(2,1)S(1)}, u32[]{:S(2)}, u32[]{:S(2)}) collective-permute-start(bf16[192,768]{1,0:T(8,128)(2,1)S(1)} %choose.1.refs_1_), channel_id=1, source_target_pairs={{0,8},{1,9},{18,26},{19,27},{4,12},{5,13},{22,30},{23,31},{8,0},{9... | collective-permute-start | bytes 884744 | tf_op jit(solution)/shard_map/ppermute | solution.py:1199
  40.5 24.2 %collective-permute-start.7 = (bf16[192,768]{1,0:T(8,128)(2,1)S(1)}, bf16[192,768]{1,0:T(8,128)(2,1)S(1)}, u32[]{:S(2)}, u32[]{:S(2)}) collective-permute-start(bf16[192,768]{1,0:T(8,128)(2,1)S(1)} %choose.1.refs_1_), channel_id=1, source_target_pairs={{0,2},{1,3},{18,16},{19,17},{4,6},{5,7},{22,20},{23,21},{8,10},{9,... | collective-permute-start | bytes 884744 | tf_op jit(solution)/shard_map/ppermute | solution.py:1340
  53.3 15.6 %collective-permute-start.10 = (bf16[192,768]{1,0:T(8,128)(2,1)S(1)}, bf16[192,768]{1,0:T(8,128)(2,1)S(1)}, u32[]{:S(2)}, u32[]{:S(2)}) collective-permute-start(bf16[192,768]{1,0:T(8,128)(2,1)S(1)} %collective-permute-done.6.refs_4_), channel_id=1, source_target_pairs={{0,2},{1,3},{18,16},{19,17},{4,6},{5,7},{22,20},{23,21},{8,10},{9,... | collective-permute-start | bytes 884744 | tf_op jit(solution)/shard_map/ppermute | solution.py:1340
  57.9 8.7 %collective-permute-start.8 = (bf16[192,768]{1,0:T(8,128)(2,1)S(1)}, bf16[192,768]{1,0:T(8,128)(2,1)S(1)}, u32[]{:S(2)}, u32[]{:S(2)}) collective-permute-start(bf16[192,768]{1,0:T(8,128)(2,1)S(1)} %collective-permute-done.4.refs_2_), channel_id=1, source_target_pairs={{0,2},{1,3},{18,16},{19,17},{4,6},{5,7},{22,20},{23,21},{8,10},{9,... | collective-permute-start | bytes 884744 | tf_op jit(solution)/shard_map/ppermute | solution.py:1340
  86.7 30.7 %collective-permute-start.21 = (bf16[768,1536]{1,0:T(8,128)(2,1)S(1)}, bf16[768,1536]{1,0:T(8,128)(2,1)}, u32[]{:S(2)}, u32[]{:S(2)}) collective-permute-start(bf16[768,1536]{1,0:T(8,128)(2,1)S(1)} %join.3.refs_1_), channel_id=1, source_target_pairs={{0,2},{1,3},{18,16},{19,17},{4,6},{5,7},{22,20},{23,21},{8,10},{9,... | collective-permute-start | bytes 7077896 | tf_op jit(solution)/shard_map/ppermute | solution.py:1211
  97.0 11.7 %collective-permute-start.17 = (bf16[272,768]{1,0:T(8,128)(2,1)S(1)}, bf16[272,768]{1,0:T(8,128)(2,1)S(1)}, u32[]{:S(2)}, u32[]{:S(2)}) collective-permute-start(bf16[272,768]{1,0:T(8,128)(2,1)S(1)} %pair_sum.8.refs_7_), channel_id=1, source_target_pairs={{0,1},{1,0},{2,3},{3,2},{4,5},{5,4},{6,7},{7,6},{8,9},{9,8},{10,11... | collective-permute-start | bytes 1253384 | tf_op jit(solution)/shard_map/ppermute | solution.py:152
  112.5 6.8 %collective-permute-start.18 = (bf16[256,768]{1,0:T(8,128)(2,1)S(1)}, bf16[256,768]{1,0:T(8,128)(2,1)S(1)}, u32[]{:S(2)}, u32[]{:S(2)}) collective-permute-start(bf16[256,768]{1,0:T(8,128)(2,1)S(1)} %get-tuple-element.174.refs_0_.refs_3_), channel_id=1, source_target_pairs={{0,16},{16,0},{1,17},{17,1},{2,18},{18,2},{3,19},{19,3},{4,20},{20... | collective-permute-start | bytes 1179656 | tf_op jit(solution)/shard_map/ppermute | solution.py:148
  112.6 11.5 %collective-permute-start.23 = (bf16[256,768]{1,0:T(8,128)(2,1)S(1)}, bf16[256,768]{1,0:T(8,128)(2,1)S(1)}, u32[]{:S(2)}, u32[]{:S(2)}) collective-permute-start(bf16[256,768]{1,0:T(8,128)(2,1)S(1)} %get-tuple-element.174.refs_0_.refs_3_), channel_id=1, source_target_pairs={{0,1},{1,0},{2,3},{3,2},{4,5},{5,4},{6,7},{7,6},{8,9},{9,8},{10,11... | collective-permute-start | bytes 1179656 | tf_op jit(solution)/shard_map/ppermute | solution.py:152
  134.1 6.3 %collective-permute-start.27 = (bf16[768,768]{1,0:T(8,128)(2,1)S(1)}, bf16[768,768]{1,0:T(8,128)(2,1)S(1)}, u32[]{:S(2)}, u32[]{:S(2)}) collective-permute-start(bf16[768,768]{1,0:T(8,128)(2,1)S(1)} %hold.18.refs_1_), channel_id=1, source_target_pairs={{0,16},{16,0},{1,17},{17,1},{2,18},{18,2},{3,19},{19,3},{4,20},{20... | collective-permute-start | bytes 3538952 | tf_op jit(solution)/shard_map/ppermute | solution.py:148
  136.4 19.0 %collective-permute-start.30 = (bf16[768,768]{1,0:T(8,128)(2,1)S(1)}, bf16[768,768]{1,0:T(8,128)(2,1)S(1)}, u32[]{:S(2)}, u32[]{:S(2)}) collective-permute-start(bf16[768,768]{1,0:T(8,128)(2,1)S(1)} %join.5.refs_1_), channel_id=1, source_target_pairs={{0,2},{1,3},{18,16},{19,17},{4,6},{5,7},{22,20},{23,21},{8,10},{9,... | collective-permute-start | bytes 3538952 | tf_op jit(solution)/shard_map/ppermute | solution.py:1211
  140.1 9.3 %collective-permute-start.26 = (bf16[272,768]{1,0:T(8,128)(2,1)S(1)}, bf16[272,768]{1,0:T(8,128)(2,1)S(1)}, u32[]{:S(2)}, u32[]{:S(2)}) collective-permute-start(bf16[272,768]{1,0:T(8,128)(2,1)S(1)} %copy-done.36), channel_id=1, source_target_pairs={{0,1},{1,0},{2,3},{3,2},{4,5},{5,4},{6,7},{7,6},{8,9},{9,8},{10,11... | collective-permute-start | bytes 1253384 | tf_op jit(solution)/shard_map/ppermute | solution.py:152
  140.2 9.2 %collective-permute-start.22 = (bf16[272,768]{1,0:T(8,128)(2,1)S(1)}, bf16[272,768]{1,0:T(8,128)(2,1)S(1)}, u32[]{:S(2)}, u32[]{:S(2)}) collective-permute-start(bf16[272,768]{1,0:T(8,128)(2,1)S(1)} %copy-done.82), channel_id=1, source_target_pairs={{0,16},{16,0},{1,17},{17,1},{2,18},{18,2},{3,19},{19,3},{4,20},{20... | collective-permute-start | bytes 1253384 | tf_op jit(solution)/shard_map/ppermute | solution.py:148
  150.3 5.7 %collective-permute-start.28 = (bf16[256,768]{1,0:T(8,128)(2,1)S(1)}, bf16[256,768]{1,0:T(8,128)(2,1)S(1)}, u32[]{:S(2)}, u32[]{:S(2)}) collective-permute-start(bf16[256,768]{1,0:T(8,128)(2,1)S(1)} %get-tuple-element.184.refs_0_.refs_2_), channel_id=1, source_target_pairs={{0,16},{16,0},{1,17},{17,1},{2,18},{18,2},{3,19},{19,3},{4,20},{20... | collective-permute-start | bytes 1179656 | tf_op jit(solution)/shard_map/ppermute | solution.py:148
  150.4 11.5 %collective-permute-start.31 = (bf16[256,768]{1,0:T(8,128)(2,1)S(1)}, bf16[256,768]{1,0:T(8,128)(2,1)S(1)}, u32[]{:S(2)}, u32[]{:S(2)}) collective-permute-start(bf16[256,768]{1,0:T(8,128)(2,1)S(1)} %get-tuple-element.184.refs_0_.refs_2_), channel_id=1, source_target_pairs={{0,1},{1,0},{2,3},{3,2},{4,5},{5,4},{6,7},{7,6},{8,9},{9,8},{10,11... | collective-permute-start | bytes 1179656 | tf_op jit(solution)/shard_map/ppermute | solution.py:152
  150.8 32.9 %collective-permute-start.38 = (bf16[768,1536]{1,0:T(8,128)(2,1)S(1)}, bf16[768,1536]{1,0:T(8,128)(2,1)S(1)}, u32[]{:S(2)}, u32[]{:S(2)}) collective-permute-start(bf16[768,1536]{1,0:T(8,128)(2,1)S(1)} %join.4.refs_1_.refs_2_), channel_id=1, source_target_pairs={{0,2},{1,3},{18,16},{19,17},{4,6},{5,7},{22,20},{23,21},{8,10},{9,... | collective-permute-start | bytes 7077896 | tf_op jit(solution)/shard_map/ppermute | solution.py:1211
  170.8 11.7 %collective-permute-start.35 = (bf16[272,768]{1,0:T(8,128)(2,1)S(1)}, bf16[272,768]{1,0:T(8,128)(2,1)S(1)}, u32[]{:S(2)}, u32[]{:S(2)}) collective-permute-start(bf16[272,768]{1,0:T(8,128)(2,1)S(1)} %pair_sum.10.refs_7_), channel_id=1, source_target_pairs={{0,1},{1,0},{2,3},{3,2},{4,5},{5,4},{6,7},{7,6},{8,9},{9,8},{10,11... | collective-permute-start | bytes 1253384 | tf_op jit(solution)/shard_map/ppermute | solution.py:152
  175.3 7.2 %collective-permute-start.34 = (bf16[272,768]{1,0:T(8,128)(2,1)S(1)}, bf16[272,768]{1,0:T(8,128)(2,1)S(1)}, u32[]{:S(2)}, u32[]{:S(2)}) collective-permute-start(bf16[272,768]{1,0:T(8,128)(2,1)S(1)} %get-tuple-element.189), channel_id=1, source_target_pairs={{0,16},{16,0},{1,17},{17,1},{2,18},{18,2},{3,19},{19,3},{4,20},{20... | collective-permute-start | bytes 1253384 | tf_op jit(solution)/shard_map/ppermute | solution.py:148
  175.4 9.0 %collective-permute-start.37 = (bf16[256,768]{1,0:T(8,128)(2,1)S(1)}, bf16[256,768]{1,0:T(8,128)(2,1)S(1)}, u32[]{:S(2)}, u32[]{:S(2)}) collective-permute-start(bf16[256,768]{1,0:T(8,128)(2,1)S(1)} %copy-done.15), channel_id=1, source_target_pairs={{0,16},{16,0},{1,17},{17,1},{2,18},{18,2},{3,19},{19,3},{4,20},{20... | collective-permute-start | bytes 1179656 | tf_op jit(solution)/shard_map/ppermute | solution.py:148
  175.9 19.1 %collective-permute-start.42 = (bf16[256,768]{1,0:T(8,128)(2,1)S(1)}, bf16[256,768]{1,0:T(8,128)(2,1)S(1)}, u32[]{:S(2)}, u32[]{:S(2)}) collective-permute-start(bf16[256,768]{1,0:T(8,128)(2,1)S(1)} %copy-done.7), channel_id=1, source_target_pairs={{0,16},{16,0},{1,17},{17,1},{2,18},{18,2},{3,19},{19,3},{4,20},{20... | collective-permute-start | bytes 1179656 | tf_op jit(solution)/shard_map/ppermute | solution.py:148
  183.3 11.5 %collective-permute-start.40 = (bf16[256,768]{1,0:T(8,128)(2,1)S(1)}, bf16[256,768]{1,0:T(8,128)(2,1)S(1)}, u32[]{:S(2)}, u32[]{:S(2)}) collective-permute-start(bf16[256,768]{1,0:T(8,128)(2,1)S(1)} %get-tuple-element.191.refs_0_), channel_id=1, source_target_pairs={{0,1},{1,0},{2,3},{3,2},{4,5},{5,4},{6,7},{7,6},{8,9},{9,8},{10,11... | collective-permute-start | bytes 1179656 | tf_op jit(solution)/shard_map/ppermute | solution.py:152
  208.7 11.2 %collective-permute-start.49 = (bf16[256,768]{1,0:T(8,128)(2,1)S(1)}, bf16[256,768]{1,0:T(8,128)(2,1)S(1)}, u32[]{:S(2)}, u32[]{:S(2)}) collective-permute-start(bf16[256,768]{1,0:T(8,128)(2,1)S(1)} %pair_sum.12.refs_7_), channel_id=1, source_target_pairs={{0,1},{1,0},{2,3},{3,2},{4,5},{5,4},{6,7},{7,6},{8,9},{9,8},{10,11... | collective-permute-start | bytes 1179656 | tf_op jit(solution)/shard_map/ppermute | solution.py:152
  211.4 8.5 %collective-permute-start.48 = (bf16[256,768]{1,0:T(8,128)(2,1)S(1)}, bf16[256,768]{1,0:T(8,128)(2,1)S(1)}, u32[]{:S(2)}, u32[]{:S(2)}) collective-permute-start(bf16[256,768]{1,0:T(8,128)(2,1)S(1)} %get-tuple-element.205), channel_id=1, source_target_pairs={{0,16},{16,0},{1,17},{17,1},{2,18},{18,2},{3,19},{19,3},{4,20},{20... | collective-permute-start | bytes 1179656 | tf_op jit(solution)/shard_map/ppermute | solution.py:148
  221.1 7.7 %collective-permute-start.50 = (bf16[272,768]{1,0:T(8,128)(2,1)S(1)}, bf16[272,768]{1,0:T(8,128)(2,1)S(1)}, u32[]{:S(2)}, u32[]{:S(2)}) collective-permute-start(bf16[272,768]{1,0:T(8,128)(2,1)S(1)} %get-tuple-element.210.refs_0_.refs_12_.refs_6_), channel_id=1, source_target_pairs={{0,16},{16,0},{1,17},{17,1},{2,18},{18,2},{3,19},{19,3},{4,20},{20... | collective-permute-start | bytes 1253384 | tf_op jit(solution)/shard_map/ppermute | solution.py:148
  221.1 12.1 %collective-permute-start.51 = (bf16[272,768]{1,0:T(8,128)(2,1)S(1)}, bf16[272,768]{1,0:T(8,128)(2,1)S(1)}, u32[]{:S(2)}, u32[]{:S(2)}) collective-permute-start(bf16[272,768]{1,0:T(8,128)(2,1)S(1)} %get-tuple-element.210.refs_0_.refs_12_.refs_6_), channel_id=1, source_target_pairs={{0,1},{1,0},{2,3},{3,2},{4,5},{5,4},{6,7},{7,6},{8,9},{9,8},{10,11... | collective-permute-start | bytes 1253384 | tf_op jit(solution)/shard_map/ppermute | solution.py:152
  224.4 31.9 %collective-permute-start.64 = (bf16[768,1536]{1,0:T(8,128)(2,1)S(1)}, bf16[768,1536]{1,0:T(8,128)(2,1)S(1)}, u32[]{:S(2)}, u32[]{:S(2)}) collective-permute-start(bf16[768,1536]{1,0:T(8,128)(2,1)S(1)} %grads.4.refs_2_.refs_1_), channel_id=1, source_target_pairs={{2,0},{3,1},{16,18},{17,19},{6,4},{7,5},{20,22},{21,23},{10,8},{11... | collective-permute-start | bytes 7077896 | tf_op jit(solution)/shard_map/ppermute | solution.py:1298
  225.7 7.7 %collective-permute-start.43 = (bf16[272,768]{1,0:T(8,128)(2,1)S(1)}, bf16[272,768]{1,0:T(8,128)(2,1)S(1)}, u32[]{:S(2)}, u32[]{:S(2)}) collective-permute-start(bf16[272,768]{1,0:T(8,128)(2,1)S(1)} %get-tuple-element.198), channel_id=1, source_target_pairs={{0,16},{16,0},{1,17},{17,1},{2,18},{18,2},{3,19},{19,3},{4,20},{20... | collective-permute-start | bytes 1253384 | tf_op jit(solution)/shard_map/ppermute | solution.py:148
  233.5 15.3 %collective-permute-start.44 = (bf16[272,768]{1,0:T(8,128)(2,1)S(1)}, bf16[272,768]{1,0:T(8,128)(2,1)S(1)}, u32[]{:S(2)}, u32[]{:S(2)}) collective-permute-start(bf16[272,768]{1,0:T(8,128)(2,1)S(1)} %pair_sum.11.refs_7_), channel_id=1, source_target_pairs={{0,1},{1,0},{2,3},{3,2},{4,5},{5,4},{6,7},{7,6},{8,9},{9,8},{10,11... | collective-permute-start | bytes 1253384 | tf_op jit(solution)/shard_map/ppermute | solution.py:152
  251.6 11.2 %collective-permute-start.55 = (bf16[256,768]{1,0:T(8,128)(2,1)S(1)}, bf16[256,768]{1,0:T(8,128)(2,1)S(1)}, u32[]{:S(2)}, u32[]{:S(2)}) collective-permute-start(bf16[256,768]{1,0:T(8,128)(2,1)S(1)} %pair_sum.13.refs_6_.refs_12_), channel_id=1, source_target_pairs={{0,1},{1,0},{2,3},{3,2},{4,5},{5,4},{6,7},{7,6},{8,9},{9,8},{10,11... | collective-permute-start | bytes 1179656 | tf_op jit(solution)/shard_map/ppermute | solution.py:152
  253.0 9.8 %collective-permute-start.54 = (bf16[256,768]{1,0:T(8,128)(2,1)S(1)}, bf16[256,768]{1,0:T(8,128)(2,1)S(1)}, u32[]{:S(2)}, u32[]{:S(2)}) collective-permute-start(bf16[256,768]{1,0:T(8,128)(2,1)S(1)} %get-tuple-element.226), channel_id=1, source_target_pairs={{0,16},{16,0},{1,17},{17,1},{2,18},{18,2},{3,19},{19,3},{4,20},{20... | collective-permute-start | bytes 1179656 | tf_op jit(solution)/shard_map/ppermute | solution.py:148
  255.0 18.1 %collective-permute-start.62 = (bf16[768,768]{1,0:T(8,128)(2,1)S(1)}, bf16[768,768]{1,0:T(8,128)(2,1)S(1)}, u32[]{:S(2)}, u32[]{:S(2)}) collective-permute-start(bf16[768,768]{1,0:T(8,128)(2,1)S(1)} %grads.5.refs_2_.refs_10_.refs_1_), channel_id=1, source_target_pairs={{2,0},{3,1},{16,18},{17,19},{6,4},{7,5},{20,22},{21,23},{10,8},{11... | collective-permute-start | bytes 3538952 | tf_op jit(solution)/shard_map/ppermute | solution.py:1298
  257.5 18.6 %collective-permute-start.65 = (bf16[384,1536]{1,0:T(8,128)(2,1)S(1)}, bf16[384,1536]{1,0:T(8,128)(2,1)S(1)}, u32[]{:S(2)}, u32[]{:S(2)}) collective-permute-start(bf16[384,1536]{1,0:T(8,128)(2,1)S(1)} %get-tuple-element.242), channel_id=1, source_target_pairs={{0,4},{1,5},{18,22},{19,23},{4,0},{5,1},{22,18},{23,19},{8,12},{9,... | collective-permute-start | bytes 3538952 | tf_op jit(solution)/shard_map/ppermute | solution.py:1199
  263.9 12.1 %collective-permute-start.61 = (bf16[272,768]{1,0:T(8,128)(2,1)S(1)}, bf16[272,768]{1,0:T(8,128)(2,1)S(1)}, u32[]{:S(2)}, u32[]{:S(2)}) collective-permute-start(bf16[272,768]{1,0:T(8,128)(2,1)S(1)} %get-tuple-element.235.refs_0_.refs_6_), channel_id=1, source_target_pairs={{0,1},{1,0},{2,3},{3,2},{4,5},{5,4},{6,7},{7,6},{8,9},{9,8},{10,11... | collective-permute-start | bytes 1253384 | tf_op jit(solution)/shard_map/ppermute | solution.py:152
  265.2 20.5 %collective-permute-start.56 = (bf16[768,768]{1,0:T(8,128)(2,1)S(1)}, bf16[768,768]{1,0:T(8,128)(2,1)S(1)}, u32[]{:S(2)}, u32[]{:S(2)}) collective-permute-start(bf16[768,768]{1,0:T(8,128)(2,1)S(1)} %pack.1.refs_1_.refs_6_.refs_2_), channel_id=1, source_target_pairs={{2,0},{3,1},{16,18},{17,19},{6,4},{7,5},{20,22},{21,23},{10,8},{11... | collective-permute-start | bytes 3538952 | tf_op jit(solution)/shard_map/ppermute | solution.py:1433
  280.5 11.8 %collective-permute-start.68 = (bf16[384,768]{1,0:T(8,128)(2,1)S(1)}, bf16[384,768]{1,0:T(8,128)(2,1)S(1)}, u32[]{:S(2)}, u32[]{:S(2)}) collective-permute-start(bf16[384,768]{1,0:T(8,128)(2,1)S(1)} %get-tuple-element.249), channel_id=1, source_target_pairs={{0,4},{1,5},{18,22},{19,23},{4,0},{5,1},{22,18},{23,19},{8,12},{9,... | collective-permute-start | bytes 1769480 | tf_op jit(solution)/shard_map/ppermute | solution.py:1199
  283.4 9.0 %collective-permute-start.60 = (bf16[256,768]{1,0:T(8,128)(2,1)S(1)}, bf16[256,768]{1,0:T(8,128)(2,1)S(1)}, u32[]{:S(2)}, u32[]{:S(2)}) collective-permute-start(bf16[256,768]{1,0:T(8,128)(2,1)S(1)} %get-tuple-element.237), channel_id=1, source_target_pairs={{0,16},{16,0},{1,17},{17,1},{2,18},{18,2},{3,19},{19,3},{4,20},{20... | collective-permute-start | bytes 1179656 | tf_op jit(solution)/shard_map/ppermute | solution.py:148
  283.7 11.6 %collective-permute-start.67 = (bf16[256,768]{1,0:T(8,128)(2,1)S(1)}, bf16[256,768]{1,0:T(8,128)(2,1)S(1)}, u32[]{:S(2)}, u32[]{:S(2)}) collective-permute-start(bf16[256,768]{1,0:T(8,128)(2,1)S(1)} %pair_sum.14), channel_id=1, source_target_pairs={{0,1},{1,0},{2,3},{3,2},{4,5},{5,4},{6,7},{7,6},{8,9},{9,8},{10,11... | collective-permute-start | bytes 1179656 | tf_op jit(solution)/shard_map/ppermute | solution.py:152
  285.2 27.5 %collective-permute-start.57 = (bf16[768,768]{1,0:T(8,128)(2,1)S(1)}, bf16[768,768]{1,0:T(8,128)(2,1)S(1)}, u32[]{:S(2)}, u32[]{:S(2)}) collective-permute-start(bf16[768,768]{1,0:T(8,128)(2,1)S(1)} %pack.1.refs_1_.refs_6_.refs_2_), channel_id=1, source_target_pairs={{0,16},{16,0},{1,17},{17,1},{2,18},{18,2},{3,19},{19,3},{4,20},{20... | collective-permute-start | bytes 3538952 | tf_op jit(solution)/shard_map/ppermute | solution.py:148
  285.7 29.8 %collective-permute-start.58 = (bf16[768,768]{1,0:T(8,128)(2,1)S(1)}, bf16[768,768]{1,0:T(8,128)(2,1)S(1)}, u32[]{:S(2)}, u32[]{:S(2)}) collective-permute-start(bf16[768,768]{1,0:T(8,128)(2,1)S(1)} %collective-permute-done.56.refs_2_), channel_id=1, source_target_pairs={{0,16},{16,0},{1,17},{17,1},{2,18},{18,2},{3,19},{19,3},{4,20},{20... | collective-permute-start | bytes 3538952 | tf_op jit(solution)/shard_map/ppermute | solution.py:148
  296.4 6.1 %collective-permute-start.69 = (bf16[272,768]{1,0:T(8,128)(2,1)S(1)}, bf16[272,768]{1,0:T(8,128)(2,1)S(1)}, u32[]{:S(2)}, u32[]{:S(2)}) collective-permute-start(bf16[272,768]{1,0:T(8,128)(2,1)S(1)} %get-tuple-element.251.refs_0_.refs_12_.refs_6_), channel_id=1, source_target_pairs={{0,16},{16,0},{1,17},{17,1},{2,18},{18,2},{3,19},{19,3},{4,20},{20... | collective-permute-start | bytes 1253384 | tf_op jit(solution)/shard_map/ppermute | solution.py:148
  296.4 12.1 %collective-permute-start.70 = (bf16[272,768]{1,0:T(8,128)(2,1)S(1)}, bf16[272,768]{1,0:T(8,128)(2,1)S(1)}, u32[]{:S(2)}, u32[]{:S(2)}) collective-permute-start(bf16[272,768]{1,0:T(8,128)(2,1)S(1)} %get-tuple-element.251.refs_0_.refs_12_.refs_6_), channel_id=1, source_target_pairs={{0,1},{1,0},{2,3},{3,2},{4,5},{5,4},{6,7},{7,6},{8,9},{9,8},{10,11... | collective-permute-start | bytes 1253384 | tf_op jit(solution)/shard_map/ppermute | solution.py:152
  300.7 39.2 %collective-permute-start.85 = (bf16[768,1536]{1,0:T(8,128)(2,1)S(1)}, bf16[768,1536]{1,0:T(8,128)(2,1)S(1)}, u32[]{:S(2)}, u32[]{:S(2)}) collective-permute-start(bf16[768,1536]{1,0:T(8,128)(2,1)S(1)} %grads.6.refs_2_.refs_1_), channel_id=1, source_target_pairs={{2,0},{3,1},{16,18},{17,19},{6,4},{7,5},{20,22},{21,23},{10,8},{11... | collective-permute-start | bytes 7077896 | tf_op jit(solution)/shard_map/ppermute | solution.py:1298
  308.5 8.6 %collective-permute-start.71 = (bf16[272,768]{1,0:T(8,128)(2,1)S(1)}, bf16[272,768]{1,0:T(8,128)(2,1)S(1)}, u32[]{:S(2)}, u32[]{:S(2)}) collective-permute-start(bf16[272,768]{1,0:T(8,128)(2,1)S(1)} %hold.28.refs_0_.refs_8_), channel_id=1, source_target_pairs={{0,16},{16,0},{1,17},{17,1},{2,18},{18,2},{3,19},{19,3},{4,20},{20... | collective-permute-start | bytes 1253384 | tf_op jit(solution)/shard_map/ppermute | solution.py:148
  308.6 23.2 %collective-permute-start.72 = (bf16[192,1536]{1,0:T(8,128)(2,1)S(1)}, bf16[192,1536]{1,0:T(8,128)(2,1)S(1)}, u32[]{:S(2)}, u32[]{:S(2)}) collective-permute-start(bf16[192,1536]{1,0:T(8,128)(2,1)S(1)} %get-tuple-element.263), channel_id=1, source_target_pairs={{0,8},{1,9},{18,26},{19,27},{4,12},{5,13},{22,30},{23,31},{8,0},{9... | collective-permute-start | bytes 1769480 | tf_op jit(solution)/shard_map/ppermute | solution.py:1199
  312.7 21.2 %collective-permute-start.73 = (bf16[192,768]{1,0:T(8,128)(2,1)S(1)}, bf16[192,768]{1,0:T(8,128)(2,1)S(1)}, u32[]{:S(2)}, u32[]{:S(2)}) collective-permute-start(bf16[192,768]{1,0:T(8,128)(2,1)S(1)} %get-tuple-element.264), channel_id=1, source_target_pairs={{0,8},{1,9},{18,26},{19,27},{4,12},{5,13},{22,30},{23,31},{8,0},{9... | collective-permute-start | bytes 884744 | tf_op jit(solution)/shard_map/ppermute | solution.py:1199
  338.7 20.8 %collective-permute-start.79 = (bf16[768,768]{1,0:T(8,128)(2,1)S(1)}, bf16[768,768]{1,0:T(8,128)(2,1)S(1)}, u32[]{:S(2)}, u32[]{:S(2)}) collective-permute-start(bf16[768,768]{1,0:T(8,128)(2,1)S(1)} %grads.7.refs_2_.refs_6_.refs_1_.refs_3_), channel_id=1, source_target_pairs={{2,0},{3,1},{16,18},{17,19},{6,4},{7,5},{20,22},{21,23},{10,8},{11... | collective-permute-start | bytes 3538952 | tf_op jit(solution)/shard_map/ppermute | solution.py:1298
  341.1 19.2 %collective-permute-start.86 = (bf16[384,1536]{1,0:T(8,128)(2,1)S(1)}, bf16[384,1536]{1,0:T(8,128)(2,1)S(1)}, u32[]{:S(2)}, u32[]{:S(2)}) collective-permute-start(bf16[384,1536]{1,0:T(8,128)(2,1)S(1)} %get-tuple-element.294), channel_id=1, source_target_pairs={{0,4},{1,5},{18,22},{19,23},{4,0},{5,1},{22,18},{23,19},{8,12},{9,... | collective-permute-start | bytes 3538952 | tf_op jit(solution)/shard_map/ppermute | solution.py:1199
  343.3 13.3 %collective-permute-start.76 = (bf16[256,768]{1,0:T(8,128)(2,1)S(1)}, bf16[256,768]{1,0:T(8,128)(2,1)S(1)}, u32[]{:S(2)}, u32[]{:S(2)}) collective-permute-start(bf16[256,768]{1,0:T(8,128)(2,1)S(1)} %pair_sum.15.refs_6_.refs_12_), channel_id=1, source_target_pairs={{0,1},{1,0},{2,3},{3,2},{4,5},{5,4},{6,7},{7,6},{8,9},{9,8},{10,11... | collective-permute-start | bytes 1179656 | tf_op jit(solution)/shard_map/ppermute | solution.py:152
  345.2 11.4 %collective-permute-start.75 = (bf16[256,768]{1,0:T(8,128)(2,1)S(1)}, bf16[256,768]{1,0:T(8,128)(2,1)S(1)}, u32[]{:S(2)}, u32[]{:S(2)}) collective-permute-start(bf16[256,768]{1,0:T(8,128)(2,1)S(1)} %get-tuple-element.268), channel_id=1, source_target_pairs={{0,16},{16,0},{1,17},{17,1},{2,18},{18,2},{3,19},{19,3},{4,20},{20... | collective-permute-start | bytes 1179656 | tf_op jit(solution)/shard_map/ppermute | solution.py:148
  347.2 8.2 %collective-permute-start.81 = (f32[8,768]{1,0:T(8,128)S(1)}, f32[8,768]{1,0:T(8,128)S(1)}, u32[]{:S(2)}, u32[]{:S(2)}) collective-permute-start(f32[8,768]{1,0:T(8,128)S(1)} %outer.1.refs_1_), channel_id=1, source_target_pairs={{0,1},{1,0},{2,3},{3,2},{4,5},{5,4},{6,7},{7,6},{8,9},{9,8},{10,11... | collective-permute-start | bytes 73736 | tf_op jit(solution)/shard_map/ppermute | solution.py:152
  360.6 19.1 %collective-permute-start.87 = (bf16[192,1536]{1,0:T(8,128)(2,1)S(1)}, bf16[192,1536]{1,0:T(8,128)(2,1)S(1)}, u32[]{:S(2)}, u32[]{:S(2)}) collective-permute-start(bf16[192,1536]{1,0:T(8,128)(2,1)S(1)} %get-tuple-element.296), channel_id=1, source_target_pairs={{0,8},{1,9},{18,26},{19,27},{4,12},{5,13},{22,30},{23,31},{8,0},{9... | collective-permute-start | bytes 1769480 | tf_op jit(solution)/shard_map/ppermute | solution.py:1199
  364.4 18.7 %collective-permute-start.83 = (bf16[432,768]{1,0:T(8,128)(2,1)S(1)}, bf16[432,768]{1,0:T(8,128)(2,1)S(1)}, u32[]{:S(2)}, u32[]{:S(2)}) collective-permute-start(bf16[432,768]{1,0:T(8,128)(2,1)S(1)} %get-tuple-element.288), channel_id=1, source_target_pairs={{0,4},{1,5},{18,22},{19,23},{4,0},{5,1},{22,18},{23,19},{8,12},{9,... | collective-permute-start | bytes 1990664 | tf_op jit(solution)/shard_map/ppermute | solution.py:1199
  367.5 24.3 %collective-permute-start.89 = (bf16[192,1536]{1,0:T(8,128)(2,1)S(1)}, bf16[192,1536]{1,0:T(8,128)(2,1)S(1)}, u32[]{:S(2)}, u32[]{:S(2)}) collective-permute-start(bf16[192,1536]{1,0:T(8,128)(2,1)S(1)} %total.3.refs_6_.refs_3_), channel_id=1, source_target_pairs={{0,16},{16,0},{1,17},{17,1},{2,18},{18,2},{3,19},{19,3},{4,20},{20... | collective-permute-start | bytes 1769480 | tf_op jit(solution)/shard_map/ppermute | solution.py:148
  379.9 12.0 %collective-permute-start.88 = (bf16[192,1536]{1,0:T(8,128)(2,1)S(1)}, bf16[192,1536]{1,0:T(8,128)(2,1)S(1)}, u32[]{:S(2)}, u32[]{:S(2)}) collective-permute-start(bf16[192,1536]{1,0:T(8,128)(2,1)S(1)} %total.5.refs_1_), channel_id=1, source_target_pairs={{0,16},{16,0},{1,17},{17,1},{2,18},{18,2},{3,19},{19,3},{4,20},{20... | collective-permute-start | bytes 1769480 | tf_op jit(solution)/shard_map/ppermute | solution.py:148
  380.6 9.7 %collective-permute-start.78 = (bf16[256,768]{1,0:T(8,128)(2,1)S(1)}, bf16[256,768]{1,0:T(8,128)(2,1)S(1)}, u32[]{:S(2)}, u32[]{:S(2)}) collective-permute-start(bf16[256,768]{1,0:T(8,128)(2,1)S(1)} %first_norm_back.3.refs_6_), channel_id=1, source_target_pairs={{2,0},{3,1},{18,2},{19,3},{6,4},{7,5},{22,6},{23,7},{10,8},{11,9},... | collective-permute-start | bytes 1179656 | tf_op jit(solution)/shard_map/ppermute | solution.py:1171
  383.2 13.2 %collective-permute-start.84 = (bf16[240,768]{1,0:T(8,128)(2,1)S(1)}, bf16[240,768]{1,0:T(8,128)(2,1)S(1)}, u32[]{:S(2)}, u32[]{:S(2)}) collective-permute-start(bf16[240,768]{1,0:T(8,128)(2,1)S(1)} %get-tuple-element.291), channel_id=1, source_target_pairs={{0,8},{1,9},{18,26},{19,27},{4,12},{5,13},{22,30},{23,31},{8,0},{9... | collective-permute-start | bytes 1105928 | tf_op jit(solution)/shard_map/ppermute | solution.py:1199
  385.2 13.0 %collective-permute-start.91 = (bf16[192,768]{1,0:T(8,128)(2,1)S(1)}, bf16[192,768]{1,0:T(8,128)(2,1)S(1)}, u32[]{:S(2)}, u32[]{:S(2)}) collective-permute-start(bf16[192,768]{1,0:T(8,128)(2,1)S(1)} %total.4.refs_7_.refs_5_.refs_3_), channel_id=1, source_target_pairs={{0,16},{16,0},{1,17},{17,1},{2,18},{18,2},{3,19},{19,3},{4,20},{20... | collective-permute-start | bytes 884744 | tf_op jit(solution)/shard_map/ppermute | solution.py:148
  (131 other events, 569.0 us)
Sparse Core Ops, SparseCore 0:
  25.7 47.3 all-gather.2
  94.2 29.8 all-gather.4
where the time goes:
time: 417 us; the launch traced here: 409 us
  waiting for transfers between devices  148 us (35%)
  Pallas kernels  119 us (29%)
  starting transfers between devices  97 us (23%)
  local copies, waits for them, and re-layouts  26.6 us (6%)
  between operations  16.5 us (4%)
    pallas_call x97, Pallas kernels, call(): pl.pallas_call(kernel, out_shape=tuple((jax.ShapeDtypeStruct(shape, kind)...  114 us
    ppermute x16, waiting for transfers between devices, x_swap(): return lax.ppermute(x, 'mp', [(i, i ^ 1) for i in range(LANES)])  66.3 us
    ppermute x11, starting transfers between devices, along_line(): return lax.ppermute(block, ('section', 'dp', 'mp'), line_pairs(step))  39.7 us
    ppermute x11, waiting for transfers between devices, along_line(): return lax.ppermute(block, ('section', 'dp', 'mp'), line_pairs(step))  35.4 us
    ppermute x48, waiting for transfers between devices, core_swap(): return lax.ppermute(x, 'section', [(0, 1), (1, 0)])  25.1 us
    unnamed x200, local copies, waits for them, and re-layouts  24.4 us
    ppermute x3, starting transfers between devices, fetched(): return (whole, lax.ppermute(whole, BOTH, crossing))  14.4 us
    ppermute x48, starting transfers between devices, core_swap(): return lax.ppermute(x, 'section', [(0, 1), (1, 0)])  11.3 us
  transfers between devices with their start and end apart: 95, of which 47 were waited for; matrix products, arithmetic and copies ran while one was open for 1% of the time, Pallas kernels for 26%

commit v1 on v0

--- a/solution.py
+++ b/solution.py
@@ -1343,7 +1343,7 @@
         pieces = [along_dp(moved)]
         lower_first = pick(flags, pieces[0], lax.ppermute(pieces[0], BOTH, crossing))
     got = core_swap(swapped)
-    early_line = along_dp(early_block(flags, up_block, got, first, after=pieces[-1:]))
+    early_line = along_dp(early_block(flags, up_block, got, first, after=[pieces[-1], own_in]))
     late_line = along_dp(late_block(flags, got, down_block))
     coming = {}
 

time: 417 us -> 416 us (level)
  waiting for transfers between devices: 148 us -> 136 us
  starting transfers between devices: 97 us -> 106 us
    ppermute x16, starting transfers between devices: 9.04 us -> 19.5 us  [x_swap(): return lax.ppermute(x, 'mp', [(i, i ^ 1) for i in range(LANES)])]
    ppermute x16, waiting for transfers between devices: 66.3 us -> 58.7 us  [x_swap(): return lax.ppermute(x, 'mp', [(i, i ^ 1) for i in range(LANES)])]
    unnamed x200 -> x206, local copies, waits for them, and re-layouts: 24.4 us -> 26.9 us
  transfers between devices with their start and end apart: 95 -> 95, of which waited for: 47 -> 46; matrix products, arithmetic and copies ran while one was open for 1% -> 1% of each run, Pallas kernels for 26% -> 26%
where the time goes in v1:
time: 416 us; the launch traced here: 408 us
  waiting for transfers between devices  136 us (33%)
  Pallas kernels  119 us (29%)
  starting transfers between devices  106 us (25%)
  local copies, waits for them, and re-layouts  29.1 us (7%)
  between operations  16.5 us (4%)
    pallas_call x97, Pallas kernels, call(): pl.pallas_call(kernel, out_shape=tuple((jax.ShapeDtypeStruct(shape, kind)...  114 us
    ppermute x16, waiting for transfers between devices, x_swap(): return lax.ppermute(x, 'mp', [(i, i ^ 1) for i in range(LANES)])  58.7 us
    ppermute x11, starting transfers between devices, along_line(): return lax.ppermute(block, ('section', 'dp', 'mp'), line_pairs(step))  39.3 us
    ppermute x11, waiting for transfers between devices, along_line(): return lax.ppermute(block, ('section', 'dp', 'mp'), line_pairs(step))  32.6 us
    unnamed x206, local copies, waits for them, and re-layouts  26.9 us
    ppermute x48, waiting for transfers between devices, core_swap(): return lax.ppermute(x, 'section', [(0, 1), (1, 0)])  23.6 us
    ppermute x16, starting transfers between devices, x_swap(): return lax.ppermute(x, 'mp', [(i, i ^ 1) for i in range(LANES)])  19.5 us
    ppermute x3, starting transfers between devices, fetched(): return (whole, lax.ppermute(whole, BOTH, crossing))  14.4 us
  transfers between devices with their start and end apart: 95, of which 46 were waited for; matrix products, arithmetic and copies ran while one was open for 1% of the time, Pallas kernels for 26%

profile of v1, /device:TPU:0, one launch (start us, length us, event | category | flops | bytes accessed | tf_op | source)
XLA Modules:
  0.0 407.7 jit_solution(2679583194621523369)
XLA Ops:
  7.3 2.1 first_block.1
  12.4 6.9 %collective-permute-start.6 = (bf16[192,768]{1,0:T(8,128)(2,1)S(1)}, bf16[192,768]{1,0:T(8,128)(2,1)S(1)}, u32[]{:S(2)}, u32[]{:S(2)}) collective-permute-start(bf16[192,768]{1,0:T(8,128)(2,1)S(1)} %choose.1.refs_1_), channel_id=1, source_target_pairs={{0,12},{1,13},{18,30},{19,31},{4,8},{5,9},{22,26},{23,27},{8,4},{9... | collective-permute-start | bytes 884744 | tf_op jit(solution)/shard_map/ppermute | solution.py:1199
  19.3 3.1 entry.1
  27.8 1.8 collective-permute-start.11
  29.8 4.7 %collective-permute-start.4 = (bf16[192,768]{1,0:T(8,128)(2,1)S(1)}, bf16[192,768]{1,0:T(8,128)(2,1)S(1)}, u32[]{:S(2)}, u32[]{:S(2)}) collective-permute-start(bf16[192,768]{1,0:T(8,128)(2,1)S(1)} %choose.1.refs_1_), channel_id=1, source_target_pairs={{0,4},{1,5},{18,22},{19,23},{4,0},{5,1},{22,18},{23,19},{8,12},{9,... | collective-permute-start | bytes 884744 | tf_op jit(solution)/shard_map/ppermute | solution.py:1199
  34.6 3.2 collective-permute-start.5
  39.8 4.1 %collective-permute-done.refs_3_ = bf16[512,768]{1,0:T(8,128)(2,1)S(1)} collective-permute-done((bf16[512,768]{1,0:T(8,128)(2,1)}, bf16[512,768]{1,0:T(8,128)(2,1)S(1)}, u32[]{:S(2)}, u32[]{:S(2)}) %collective-permute-start) | collective-permute-done | bytes 786464 | tf_op jit(solution)/shard_map/ppermute | solution.py:1321
  43.9 2.5 collective-permute-start.13
  50.6 2.9 collective-permute-start.10
  54.8 6.1 %collective-permute-done.5.refs_3_ = bf16[192,768]{1,0:T(8,128)(2,1)S(1)} collective-permute-done((bf16[192,768]{1,0:T(8,128)(2,1)S(1)}, bf16[192,768]{1,0:T(8,128)(2,1)S(1)}, u32[]{:S(2)}, u32[]{:S(2)}) %collective-permute-start.5) | collective-permute-done | bytes 294944 | tf_op jit(solution)/shard_map/ppermute | solution.py:1199
  64.1 2.3 collective-permute-done.9.refs_7_
  70.7 5.0 %attend.4 = (f32[512,192]{1,0:T(8,128)S(1)}, bf16[272,768]{1,0:T(8,128)(2,1)S(1)}, bf16[272,768]{1,0:T(8,128)(2,1)}, f32[512,128]{1,0:T(8,128)S(1)}) custom-call(bf16[512,576]{1,0:T(8,128)(2,1)S(1)} %project.5.refs_0_.refs_2_.refs_1_, bf16[512,576]{1,0:T(8,128)(2,1)S(1)} %project.4.refs_1_.refs_0_, bf16[512,576]{1,0:T(8,128)(2,1)S(1)} %project.5.refs_0_.refs_2_.refs_1_, ...), custom_call_target="tpu_custom_call" | custom-call | flops 4000000000 | bytes 1 | tf_op jit(solution)/shard_map/attend/pallas_call | solution.py:41
  80.7 2.7 collective-permute-done.20.refs_2_
  84.2 6.0 %collective-permute-start.21 = (bf16[768,1536]{1,0:T(8,128)(2,1)S(1)}, bf16[768,1536]{1,0:T(8,128)(2,1)}, u32[]{:S(2)}, u32[]{:S(2)}) collective-permute-start(bf16[768,1536]{1,0:T(8,128)(2,1)S(1)} %join.3.refs_1_), channel_id=1, source_target_pairs={{0,2},{1,3},{18,16},{19,17},{4,6},{5,7},{22,20},{23,21},{8,10},{9,... | collective-permute-start | bytes 7077896 | tf_op jit(solution)/shard_map/ppermute | solution.py:1211
  98.3 4.2 %attend.5 = (f32[512,192]{1,0:T(8,128)S(1)}, bf16[272,768]{1,0:T(8,128)(2,1)S(1)}, bf16[272,768]{1,0:T(8,128)(2,1)S(1)}, f32[512,128]{1,0:T(8,128)S(1)}) custom-call(bf16[512,576]{1,0:T(8,128)(2,1)S(1)} %copy-done.24, bf16[512,576]{1,0:T(8,128)(2,1)S(1)} %copy-done.24, bf16[512,576]{1,0:T(8,128)(2,1)S(1)} %copy-done.52, f32[8,1024]{1,0:T(8,128)S(1)} %copy-done.27, ...), custom_call_target="tpu_custom_call" | custom-call | flops 4000000000 | bytes 1 | tf_op jit(solution)/shard_map/attend/pallas_call | solution.py:41
  104.0 2.4 collective-permute-done.17.refs_0_
  111.3 3.7 collective-permute-done.21.refs_2_
  115.0 1.9 pick.3.refs_2_.refs_5_
  116.9 1.9 feed.4
  119.6 2.0 collective-permute-done.23.refs_0_
  121.8 1.7 collective-permute-done.24.refs_1_.refs_3_
  123.5 1.9 feed.5
  133.9 3.7 collective-permute-start.30
  139.7 7.2 %collective-permute-done.26.refs_0_ = bf16[272,768]{1,0:T(8,128)(2,1)S(1)} collective-permute-done((bf16[272,768]{1,0:T(8,128)(2,1)S(1)}, bf16[272,768]{1,0:T(8,128)(2,1)S(1)}, u32[]{:S(2)}, u32[]{:S(2)}) %collective-permute-start.26) | collective-permute-done | bytes 417824 | tf_op jit(solution)/shard_map/ppermute | solution.py:152
  149.1 4.7 %collective-permute-start.38 = (bf16[768,1536]{1,0:T(8,128)(2,1)S(1)}, bf16[768,1536]{1,0:T(8,128)(2,1)S(1)}, u32[]{:S(2)}, u32[]{:S(2)}) collective-permute-start(bf16[768,1536]{1,0:T(8,128)(2,1)S(1)} %join.4.refs_1_.refs_2_), channel_id=1, source_target_pairs={{0,2},{1,3},{18,16},{19,17},{4,6},{5,7},{22,20},{23,21},{8,10},{9,... | collective-permute-start | bytes 7077896 | tf_op jit(solution)/shard_map/ppermute | solution.py:1211
  155.3 4.1 %collective-permute-done.31.refs_0_ = bf16[256,768]{1,0:T(8,128)(2,1)S(1)} collective-permute-done((bf16[256,768]{1,0:T(8,128)(2,1)S(1)}, bf16[256,768]{1,0:T(8,128)(2,1)S(1)}, u32[]{:S(2)}, u32[]{:S(2)}) %collective-permute-start.31) | collective-permute-done | bytes 393248 | tf_op jit(solution)/shard_map/ppermute | solution.py:152
  162.1 4.2 %attend.6 = (f32[512,192]{1,0:T(8,128)S(1)}, bf16[272,768]{1,0:T(8,128)(2,1)S(1)}, bf16[272,768]{1,0:T(8,128)(2,1)S(1)}, f32[512,128]{1,0:T(8,128)S(1)}) custom-call(bf16[512,576]{1,0:T(8,128)(2,1)S(1)} %project.7.refs_0_.refs_2_.refs_1_, bf16[512,576]{1,0:T(8,128)(2,1)S(1)} %project.6.refs_1_.refs_0_, bf16[512,576]{1,0:T(8,128)(2,1)S(1)} %project.7.refs_0_.refs_2_.refs_1_, ...), custom_call_target="tpu_custom_call" | custom-call | flops 4000000000 | bytes 1 | tf_op jit(solution)/shard_map/attend/pallas_call | solution.py:41
  169.5 4.2 %attend.7 = (f32[512,192]{1,0:T(8,128)S(1)}, bf16[272,768]{1,0:T(8,128)(2,1)S(1)}, bf16[272,768]{1,0:T(8,128)(2,1)S(1)}, f32[512,128]{1,0:T(8,128)S(1)}) custom-call(bf16[512,576]{1,0:T(8,128)(2,1)S(1)} %project.6.refs_1_.refs_0_, bf16[512,576]{1,0:T(8,128)(2,1)S(1)} %project.6.refs_1_.refs_0_, bf16[512,576]{1,0:T(8,128)(2,1)S(1)} %project.7.refs_0_.refs_2_.refs_1_, ...), custom_call_target="tpu_custom_call" | custom-call | flops 4000000000 | bytes 1 | tf_op jit(solution)/shard_map/attend/pallas_call | solution.py:41
  174.4 5.6 %collective-permute-done.35.refs_0_ = bf16[272,768]{1,0:T(8,128)(2,1)S(1)} collective-permute-done((bf16[272,768]{1,0:T(8,128)(2,1)S(1)}, bf16[272,768]{1,0:T(8,128)(2,1)S(1)}, u32[]{:S(2)}, u32[]{:S(2)}) %collective-permute-start.35) | collective-permute-done | bytes 417824 | tf_op jit(solution)/shard_map/ppermute | solution.py:152
  182.9 3.0 feed.6
  185.9 6.5 %collective-permute-done.40.refs_0_ = bf16[256,768]{1,0:T(8,128)(2,1)S(1)} collective-permute-done((bf16[256,768]{1,0:T(8,128)(2,1)S(1)}, bf16[256,768]{1,0:T(8,128)(2,1)S(1)}, u32[]{:S(2)}, u32[]{:S(2)}) %collective-permute-start.40) | collective-permute-done | bytes 393248 | tf_op jit(solution)/shard_map/ppermute | solution.py:152
  194.2 2.6 feed.7
  199.2 2.8 collective-permute-done.46.refs_1_
  202.0 2.3 feed_back.4
  207.5 2.3 feed_back.5
  209.9 7.6 %collective-permute-done.49.refs_0_ = bf16[256,768]{1,0:T(8,128)(2,1)S(1)} collective-permute-done((bf16[256,768]{1,0:T(8,128)(2,1)S(1)}, bf16[256,768]{1,0:T(8,128)(2,1)S(1)}, u32[]{:S(2)}, u32[]{:S(2)}) %collective-permute-start.49) | collective-permute-done | bytes 393248 | tf_op jit(solution)/shard_map/ppermute | solution.py:152
  219.9 2.9 grads.4.refs_2_.refs_1_
  224.0 3.1 collective-permute-start.43
  227.9 2.9 collective-permute-done.51.refs_0_
  233.3 13.1 %attend_back.2 = (bf16[512,576]{1,0:T(8,128)(2,1)S(1)}, bf16[512,576]{1,0:T(8,128)(2,1)S(1)}) custom-call(bf16[512,576]{1,0:T(8,128)(2,1)S(1)} %project.6.refs_1_.refs_0_, bf16[512,576]{1,0:T(8,128)(2,1)S(1)} %project.7.refs_0_.refs_2_.refs_1_, bf16[512,192]{1,0:T(8,128)(2,1)S(1)} %get-tuple-element.212.refs_1_.refs_2_, ...), custom_call_target="tpu_custom_call" | custom-call | flops 14000000000 | bytes 1 | tf_op jit(solution)/shard_map/attend_back/pallas_call | solution.py:41
  251.2 1.9 grads.5.refs_2_.refs_10_.refs_1_
  255.6 3.7 collective-permute-start.65
  264.8 2.4 feed_back.6
  267.1 4.1 %collective-permute-done.62.refs_2_ = bf16[768,768]{1,0:T(8,128)(2,1)S(1)} collective-permute-done((bf16[768,768]{1,0:T(8,128)(2,1)S(1)}, bf16[768,768]{1,0:T(8,128)(2,1)S(1)}, u32[]{:S(2)}, u32[]{:S(2)}) %collective-permute-start.62) | collective-permute-done | bytes 1179680 | tf_op jit(solution)/shard_map/ppermute | solution.py:1298
  275.4 2.4 feed_back.7
  278.0 3.2 collective-permute-start.68
  283.9 5.9 %collective-permute-done.68.refs_1_ = bf16[384,768]{1,0:T(8,128)(2,1)S(1)} collective-permute-done((bf16[384,768]{1,0:T(8,128)(2,1)S(1)}, bf16[384,768]{1,0:T(8,128)(2,1)S(1)}, u32[]{:S(2)}, u32[]{:S(2)}) %collective-permute-start.68) | collective-permute-done | bytes 589856 | tf_op jit(solution)/shard_map/ppermute | solution.py:1199
  289.9 3.0 collective-permute-done.67.refs_2_
  295.7 2.8 grads.6.refs_2_.refs_1_
  300.9 5.3 %collective-permute-done.70.refs_0_ = bf16[272,768]{1,0:T(8,128)(2,1)S(1)} collective-permute-done((bf16[272,768]{1,0:T(8,128)(2,1)S(1)}, bf16[272,768]{1,0:T(8,128)(2,1)S(1)}, u32[]{:S(2)}, u32[]{:S(2)}) %collective-permute-start.70) | collective-permute-done | bytes 417824 | tf_op jit(solution)/shard_map/ppermute | solution.py:152
  306.4 4.7 %collective-permute-start.72 = (bf16[192,1536]{1,0:T(8,128)(2,1)S(1)}, bf16[192,1536]{1,0:T(8,128)(2,1)S(1)}, u32[]{:S(2)}, u32[]{:S(2)}) collective-permute-start(bf16[192,1536]{1,0:T(8,128)(2,1)S(1)} %get-tuple-element.263), channel_id=1, source_target_pairs={{0,8},{1,9},{18,26},{19,27},{4,12},{5,13},{22,30},{23,31},{8,0},{9... | collective-permute-start | bytes 1769480 | tf_op jit(solution)/shard_map/ppermute | solution.py:1199
  311.0 2.2 collective-permute-start.73
  316.5 13.1 %attend_back.3 = (bf16[512,576]{1,0:T(8,128)(2,1)S(1)}, bf16[512,576]{1,0:T(8,128)(2,1)S(1)}) custom-call(bf16[512,576]{1,0:T(8,128)(2,1)S(1)} %copy-done.25, bf16[512,576]{1,0:T(8,128)(2,1)S(1)} %copy-done.53, bf16[512,192]{1,0:T(8,128)(2,1)S(1)} %get-tuple-element.253.refs_1_.refs_2_, bf16[512,192]{1,0:T(8,128)(2,1)S(1)} %get-tuple-element.258.refs_3_, ...), custom_call_target="tpu_custom_call" | custom-call | flops 14000000000 | bytes 1 | tf_op jit(solution)/shard_map/attend_back/pallas_call | solution.py:41
  329.8 1.9 collective-permute-done.73.refs_1_
  334.5 1.9 grads.7.refs_2_.refs_6_.refs_1_.refs_3_
  338.8 2.1 collective-permute-start.86
  345.8 7.4 %collective-permute-done.81.refs_2_ = f32[8,768]{1,0:T(8,128)S(1)} collective-permute-done((f32[8,768]{1,0:T(8,128)S(1)}, f32[8,768]{1,0:T(8,128)S(1)}, u32[]{:S(2)}, u32[]{:S(2)}) %collective-permute-start.81) | collective-permute-done | bytes 24608 | tf_op jit(solution)/shard_map/ppermute | solution.py:152
  358.5 4.2 %collective-permute-start.87 = (bf16[192,1536]{1,0:T(8,128)(2,1)S(1)}, bf16[192,1536]{1,0:T(8,128)(2,1)S(1)}, u32[]{:S(2)}, u32[]{:S(2)}) collective-permute-start(bf16[192,1536]{1,0:T(8,128)(2,1)S(1)} %get-tuple-element.296), channel_id=1, source_target_pairs={{0,8},{1,9},{18,26},{19,27},{4,12},{5,13},{22,30},{23,31},{8,0},{9... | collective-permute-start | bytes 1769480 | tf_op jit(solution)/shard_map/ppermute | solution.py:1199
  362.7 2.6 collective-permute-start.83
  365.3 12.0 %collective-permute-done.87.refs_1_ = bf16[192,1536]{1,0:T(8,128)(2,1)S(1)} collective-permute-done((bf16[192,1536]{1,0:T(8,128)(2,1)S(1)}, bf16[192,1536]{1,0:T(8,128)(2,1)S(1)}, u32[]{:S(2)}, u32[]{:S(2)}) %collective-permute-start.87) | collective-permute-done | bytes 589856 | tf_op jit(solution)/shard_map/ppermute | solution.py:1199
  379.5 1.9 collective-permute-done.83.refs_1_
  381.6 1.9 collective-permute-start.84
  384.0 3.9 collective-permute-done.78.refs_2_
  391.1 3.7 collective-permute-done.84.refs_1_
  (460 shorter events, 136.9 us)
Async XLA Ops:
  7.2 70.8 %all-gather.3.cloned.1.call-start = ((), (), s32[]{:S(2)}) async-start(), calls=%async_computation | async-start | bytes 2211840 | tf_op jit(solution)/shard_map/all_gather | solution.py:1207
  10.6 12.5 %collective-permute-start.19 = (bf16[192,1152]{1,0:T(8,128)(2,1)S(1)}, bf16[192,1152]{1,0:T(8,128)(2,1)S(1)}, u32[]{:S(2)}, u32[]{:S(2)}) collective-permute-start(bf16[192,1152]{1,0:T(8,128)(2,1)S(1)} %get-tuple-element.175), channel_id=1, source_target_pairs={{0,16},{16,0},{1,17},{17,1},{2,18},{18,2},{3,19},{19,3},{4,20},{20... | collective-permute-start | bytes 1327112 | tf_op jit(solution)/shard_map/ppermute | solution.py:148
  12.4 11.7 %collective-permute-start.6 = (bf16[192,768]{1,0:T(8,128)(2,1)S(1)}, bf16[192,768]{1,0:T(8,128)(2,1)S(1)}, u32[]{:S(2)}, u32[]{:S(2)}) collective-permute-start(bf16[192,768]{1,0:T(8,128)(2,1)S(1)} %choose.1.refs_1_), channel_id=1, source_target_pairs={{0,12},{1,13},{18,30},{19,31},{4,8},{5,9},{22,26},{23,27},{8,4},{9... | collective-permute-start | bytes 884744 | tf_op jit(solution)/shard_map/ppermute | solution.py:1199
  26.3 102.9 %all-gather.5.cloned.1.call-start = ((), (), s32[]{:S(2)}) async-start(), calls=%async_computation.1 | async-start | bytes 1474560 | tf_op jit(solution)/shard_map/all_gather | solution.py:1207
  26.3 17.6 %collective-permute-start = (bf16[512,768]{1,0:T(8,128)(2,1)}, bf16[512,768]{1,0:T(8,128)(2,1)S(1)}, u32[]{:S(2)}, u32[]{:S(2)}) collective-permute-start(bf16[512,768]{1,0:T(8,128)(2,1)} %get-tuple-element.163), channel_id=1, source_target_pairs={{0,2},{1,3},{18,16},{19,17},{4,6},{5,7},{22,20},{23,21},{8,10},{9,... | collective-permute-start | bytes 2359304 | tf_op jit(solution)/shard_map/ppermute | solution.py:1321
  27.7 10.1 %collective-permute-start.1 = (f32[4,768]{1,0:T(4,128)S(1)}, f32[4,768]{1,0:T(4,128)S(1)}, u32[]{:S(2)}, u32[]{:S(2)}) collective-permute-start(f32[4,768]{1,0:T(4,128)S(1)} %pad_maximum_fusion), channel_id=1, source_target_pairs={{0,16},{16,0},{1,17},{17,1},{2,18},{18,2},{3,19},{19,3},{4,20},{20... | collective-permute-start | bytes 36872 | tf_op jit(solution)/shard_map/ppermute | solution.py:148
  27.8 34.5 %collective-permute-start.11 = (bf16[512,768]{1,0:T(8,128)(2,1)}, bf16[512,768]{1,0:T(8,128)(2,1)S(1)}, u32[]{:S(2)}, u32[]{:S(2)}) collective-permute-start(bf16[512,768]{1,0:T(8,128)(2,1)} %copy-done.83), channel_id=1, source_target_pairs={{0,1},{1,0},{2,17},{3,16},{16,3},{17,2},{18,19},{19,18},{4,5},{5,4... | collective-permute-start | bytes 2359304 | tf_op jit(solution)/shard_map/ppermute | solution.py:1322
  29.8 23.6 %collective-permute-start.4 = (bf16[192,768]{1,0:T(8,128)(2,1)S(1)}, bf16[192,768]{1,0:T(8,128)(2,1)S(1)}, u32[]{:S(2)}, u32[]{:S(2)}) collective-permute-start(bf16[192,768]{1,0:T(8,128)(2,1)S(1)} %choose.1.refs_1_), channel_id=1, source_target_pairs={{0,4},{1,5},{18,22},{19,23},{4,0},{5,1},{22,18},{23,19},{8,12},{9,... | collective-permute-start | bytes 884744 | tf_op jit(solution)/shard_map/ppermute | solution.py:1199
  34.6 26.4 %collective-permute-start.5 = (bf16[192,768]{1,0:T(8,128)(2,1)S(1)}, bf16[192,768]{1,0:T(8,128)(2,1)S(1)}, u32[]{:S(2)}, u32[]{:S(2)}) collective-permute-start(bf16[192,768]{1,0:T(8,128)(2,1)S(1)} %choose.1.refs_1_), channel_id=1, source_target_pairs={{0,8},{1,9},{18,26},{19,27},{4,12},{5,13},{22,30},{23,31},{8,0},{9... | collective-permute-start | bytes 884744 | tf_op jit(solution)/shard_map/ppermute | solution.py:1199
  37.8 24.4 %collective-permute-start.7 = (bf16[192,768]{1,0:T(8,128)(2,1)S(1)}, bf16[192,768]{1,0:T(8,128)(2,1)S(1)}, u32[]{:S(2)}, u32[]{:S(2)}) collective-permute-start(bf16[192,768]{1,0:T(8,128)(2,1)S(1)} %choose.1.refs_1_), channel_id=1, source_target_pairs={{0,2},{1,3},{18,16},{19,17},{4,6},{5,7},{22,20},{23,21},{8,10},{9,... | collective-permute-start | bytes 884744 | tf_op jit(solution)/shard_map/ppermute | solution.py:1340
  43.9 6.7 %collective-permute-start.13 = (f32[1,1920]{1,0:T(1,128)S(1)}, f32[1,1920]{1,0:T(1,128)S(1)}, u32[]{:S(2)}, u32[]{:S(2)}) collective-permute-start(f32[1,1920]{1,0:T(1,128)S(1)} %concatenate.27), channel_id=1, source_target_pairs={{0,2},{1,3},{2,0},{3,1},{4,6},{5,7},{6,4},{7,5},{8,10},{9,11},{10,... | collective-permute-start | bytes 23048 | tf_op jit(solution)/shard_map/ppermute | solution.py:156
  50.6 15.9 %collective-permute-start.10 = (bf16[192,768]{1,0:T(8,128)(2,1)S(1)}, bf16[192,768]{1,0:T(8,128)(2,1)S(1)}, u32[]{:S(2)}, u32[]{:S(2)}) collective-permute-start(bf16[192,768]{1,0:T(8,128)(2,1)S(1)} %collective-permute-done.6.refs_4_), channel_id=1, source_target_pairs={{0,2},{1,3},{18,16},{19,17},{4,6},{5,7},{22,20},{23,21},{8,10},{9,... | collective-permute-start | bytes 884744 | tf_op jit(solution)/shard_map/ppermute | solution.py:1340
  53.5 10.6 %collective-permute-start.8 = (bf16[192,768]{1,0:T(8,128)(2,1)S(1)}, bf16[192,768]{1,0:T(8,128)(2,1)S(1)}, u32[]{:S(2)}, u32[]{:S(2)}) collective-permute-start(bf16[192,768]{1,0:T(8,128)(2,1)S(1)} %collective-permute-done.4.refs_2_), channel_id=1, source_target_pairs={{0,2},{1,3},{18,16},{19,17},{4,6},{5,7},{22,20},{23,21},{8,10},{9,... | collective-permute-start | bytes 884744 | tf_op jit(solution)/shard_map/ppermute | solution.py:1340
  84.2 30.7 %collective-permute-start.21 = (bf16[768,1536]{1,0:T(8,128)(2,1)S(1)}, bf16[768,1536]{1,0:T(8,128)(2,1)}, u32[]{:S(2)}, u32[]{:S(2)}) collective-permute-start(bf16[768,1536]{1,0:T(8,128)(2,1)S(1)} %join.3.refs_1_), channel_id=1, source_target_pairs={{0,2},{1,3},{18,16},{19,17},{4,6},{5,7},{22,20},{23,21},{8,10},{9,... | collective-permute-start | bytes 7077896 | tf_op jit(solution)/shard_map/ppermute | solution.py:1211
  94.6 11.7 %collective-permute-start.17 = (bf16[272,768]{1,0:T(8,128)(2,1)S(1)}, bf16[272,768]{1,0:T(8,128)(2,1)S(1)}, u32[]{:S(2)}, u32[]{:S(2)}) collective-permute-start(bf16[272,768]{1,0:T(8,128)(2,1)S(1)} %pair_sum.8.refs_7_), channel_id=1, source_target_pairs={{0,1},{1,0},{2,3},{3,2},{4,5},{5,4},{6,7},{7,6},{8,9},{9,8},{10,11... | collective-permute-start | bytes 1253384 | tf_op jit(solution)/shard_map/ppermute | solution.py:152
  110.1 6.8 %collective-permute-start.18 = (bf16[256,768]{1,0:T(8,128)(2,1)S(1)}, bf16[256,768]{1,0:T(8,128)(2,1)S(1)}, u32[]{:S(2)}, u32[]{:S(2)}) collective-permute-start(bf16[256,768]{1,0:T(8,128)(2,1)S(1)} %get-tuple-element.174.refs_0_.refs_3_), channel_id=1, source_target_pairs={{0,16},{16,0},{1,17},{17,1},{2,18},{18,2},{3,19},{19,3},{4,20},{20... | collective-permute-start | bytes 1179656 | tf_op jit(solution)/shard_map/ppermute | solution.py:148
  110.1 11.5 %collective-permute-start.23 = (bf16[256,768]{1,0:T(8,128)(2,1)S(1)}, bf16[256,768]{1,0:T(8,128)(2,1)S(1)}, u32[]{:S(2)}, u32[]{:S(2)}) collective-permute-start(bf16[256,768]{1,0:T(8,128)(2,1)S(1)} %get-tuple-element.174.refs_0_.refs_3_), channel_id=1, source_target_pairs={{0,1},{1,0},{2,3},{3,2},{4,5},{5,4},{6,7},{7,6},{8,9},{9,8},{10,11... | collective-permute-start | bytes 1179656 | tf_op jit(solution)/shard_map/ppermute | solution.py:152
  131.6 7.3 %collective-permute-start.27 = (bf16[768,768]{1,0:T(8,128)(2,1)S(1)}, bf16[768,768]{1,0:T(8,128)(2,1)S(1)}, u32[]{:S(2)}, u32[]{:S(2)}) collective-permute-start(bf16[768,768]{1,0:T(8,128)(2,1)S(1)} %hold.18.refs_1_), channel_id=1, source_target_pairs={{0,16},{16,0},{1,17},{17,1},{2,18},{18,2},{3,19},{19,3},{4,20},{20... | collective-permute-start | bytes 3538952 | tf_op jit(solution)/shard_map/ppermute | solution.py:148
  133.9 19.9 %collective-permute-start.30 = (bf16[768,768]{1,0:T(8,128)(2,1)S(1)}, bf16[768,768]{1,0:T(8,128)(2,1)S(1)}, u32[]{:S(2)}, u32[]{:S(2)}) collective-permute-start(bf16[768,768]{1,0:T(8,128)(2,1)S(1)} %join.5.refs_1_), channel_id=1, source_target_pairs={{0,2},{1,3},{18,16},{19,17},{4,6},{5,7},{22,20},{23,21},{8,10},{9,... | collective-permute-start | bytes 3538952 | tf_op jit(solution)/shard_map/ppermute | solution.py:1211
  137.7 9.3 %collective-permute-start.26 = (bf16[272,768]{1,0:T(8,128)(2,1)S(1)}, bf16[272,768]{1,0:T(8,128)(2,1)S(1)}, u32[]{:S(2)}, u32[]{:S(2)}) collective-permute-start(bf16[272,768]{1,0:T(8,128)(2,1)S(1)} %copy-done.36), channel_id=1, source_target_pairs={{0,1},{1,0},{2,3},{3,2},{4,5},{5,4},{6,7},{7,6},{8,9},{9,8},{10,11... | collective-permute-start | bytes 1253384 | tf_op jit(solution)/shard_map/ppermute | solution.py:152
  138.9 8.1 %collective-permute-start.22 = (bf16[272,768]{1,0:T(8,128)(2,1)S(1)}, bf16[272,768]{1,0:T(8,128)(2,1)S(1)}, u32[]{:S(2)}, u32[]{:S(2)}) collective-permute-start(bf16[272,768]{1,0:T(8,128)(2,1)S(1)} %copy-done.85), channel_id=1, source_target_pairs={{0,16},{16,0},{1,17},{17,1},{2,18},{18,2},{3,19},{19,3},{4,20},{20... | collective-permute-start | bytes 1253384 | tf_op jit(solution)/shard_map/ppermute | solution.py:148
  147.9 6.7 %collective-permute-start.28 = (bf16[256,768]{1,0:T(8,128)(2,1)S(1)}, bf16[256,768]{1,0:T(8,128)(2,1)S(1)}, u32[]{:S(2)}, u32[]{:S(2)}) collective-permute-start(bf16[256,768]{1,0:T(8,128)(2,1)S(1)} %get-tuple-element.184.refs_0_.refs_2_), channel_id=1, source_target_pairs={{0,16},{16,0},{1,17},{17,1},{2,18},{18,2},{3,19},{19,3},{4,20},{20... | collective-permute-start | bytes 1179656 | tf_op jit(solution)/shard_map/ppermute | solution.py:148
  147.9 11.5 %collective-permute-start.31 = (bf16[256,768]{1,0:T(8,128)(2,1)S(1)}, bf16[256,768]{1,0:T(8,128)(2,1)S(1)}, u32[]{:S(2)}, u32[]{:S(2)}) collective-permute-start(bf16[256,768]{1,0:T(8,128)(2,1)S(1)} %get-tuple-element.184.refs_0_.refs_2_), channel_id=1, source_target_pairs={{0,1},{1,0},{2,3},{3,2},{4,5},{5,4},{6,7},{7,6},{8,9},{9,8},{10,11... | collective-permute-start | bytes 1179656 | tf_op jit(solution)/shard_map/ppermute | solution.py:152
  149.1 32.9 %collective-permute-start.38 = (bf16[768,1536]{1,0:T(8,128)(2,1)S(1)}, bf16[768,1536]{1,0:T(8,128)(2,1)S(1)}, u32[]{:S(2)}, u32[]{:S(2)}) collective-permute-start(bf16[768,1536]{1,0:T(8,128)(2,1)S(1)} %join.4.refs_1_.refs_2_), channel_id=1, source_target_pairs={{0,2},{1,3},{18,16},{19,17},{4,6},{5,7},{22,20},{23,21},{8,10},{9,... | collective-permute-start | bytes 7077896 | tf_op jit(solution)/shard_map/ppermute | solution.py:1211
  168.3 11.7 %collective-permute-start.35 = (bf16[272,768]{1,0:T(8,128)(2,1)S(1)}, bf16[272,768]{1,0:T(8,128)(2,1)S(1)}, u32[]{:S(2)}, u32[]{:S(2)}) collective-permute-start(bf16[272,768]{1,0:T(8,128)(2,1)S(1)} %pair_sum.10.refs_7_), channel_id=1, source_target_pairs={{0,1},{1,0},{2,3},{3,2},{4,5},{5,4},{6,7},{7,6},{8,9},{9,8},{10,11... | collective-permute-start | bytes 1253384 | tf_op jit(solution)/shard_map/ppermute | solution.py:152
  173.7 6.4 %collective-permute-start.34 = (bf16[272,768]{1,0:T(8,128)(2,1)S(1)}, bf16[272,768]{1,0:T(8,128)(2,1)S(1)}, u32[]{:S(2)}, u32[]{:S(2)}) collective-permute-start(bf16[272,768]{1,0:T(8,128)(2,1)S(1)} %get-tuple-element.189), channel_id=1, source_target_pairs={{0,16},{16,0},{1,17},{17,1},{2,18},{18,2},{3,19},{19,3},{4,20},{20... | collective-permute-start | bytes 1253384 | tf_op jit(solution)/shard_map/ppermute | solution.py:148
  173.8 9.1 %collective-permute-start.37 = (bf16[256,768]{1,0:T(8,128)(2,1)S(1)}, bf16[256,768]{1,0:T(8,128)(2,1)S(1)}, u32[]{:S(2)}, u32[]{:S(2)}) collective-permute-start(bf16[256,768]{1,0:T(8,128)(2,1)S(1)} %copy-done.15), channel_id=1, source_target_pairs={{0,16},{16,0},{1,17},{17,1},{2,18},{18,2},{3,19},{19,3},{4,20},{20... | collective-permute-start | bytes 1179656 | tf_op jit(solution)/shard_map/ppermute | solution.py:148
  174.3 18.2 %collective-permute-start.42 = (bf16[256,768]{1,0:T(8,128)(2,1)S(1)}, bf16[256,768]{1,0:T(8,128)(2,1)S(1)}, u32[]{:S(2)}, u32[]{:S(2)}) collective-permute-start(bf16[256,768]{1,0:T(8,128)(2,1)S(1)} %copy-done.7), channel_id=1, source_target_pairs={{0,16},{16,0},{1,17},{17,1},{2,18},{18,2},{3,19},{19,3},{4,20},{20... | collective-permute-start | bytes 1179656 | tf_op jit(solution)/shard_map/ppermute | solution.py:148
  180.9 11.5 %collective-permute-start.40 = (bf16[256,768]{1,0:T(8,128)(2,1)S(1)}, bf16[256,768]{1,0:T(8,128)(2,1)S(1)}, u32[]{:S(2)}, u32[]{:S(2)}) collective-permute-start(bf16[256,768]{1,0:T(8,128)(2,1)S(1)} %get-tuple-element.191.refs_0_), channel_id=1, source_target_pairs={{0,1},{1,0},{2,3},{3,2},{4,5},{5,4},{6,7},{7,6},{8,9},{9,8},{10,11... | collective-permute-start | bytes 1179656 | tf_op jit(solution)/shard_map/ppermute | solution.py:152
  206.2 11.2 %collective-permute-start.49 = (bf16[256,768]{1,0:T(8,128)(2,1)S(1)}, bf16[256,768]{1,0:T(8,128)(2,1)S(1)}, u32[]{:S(2)}, u32[]{:S(2)}) collective-permute-start(bf16[256,768]{1,0:T(8,128)(2,1)S(1)} %pair_sum.12.refs_7_), channel_id=1, source_target_pairs={{0,1},{1,0},{2,3},{3,2},{4,5},{5,4},{6,7},{7,6},{8,9},{9,8},{10,11... | collective-permute-start | bytes 1179656 | tf_op jit(solution)/shard_map/ppermute | solution.py:152
  209.8 7.7 %collective-permute-start.48 = (bf16[256,768]{1,0:T(8,128)(2,1)S(1)}, bf16[256,768]{1,0:T(8,128)(2,1)S(1)}, u32[]{:S(2)}, u32[]{:S(2)}) collective-permute-start(bf16[256,768]{1,0:T(8,128)(2,1)S(1)} %get-tuple-element.205), channel_id=1, source_target_pairs={{0,16},{16,0},{1,17},{17,1},{2,18},{18,2},{3,19},{19,3},{4,20},{20... | collective-permute-start | bytes 1179656 | tf_op jit(solution)/shard_map/ppermute | solution.py:148
  218.6 8.6 %collective-permute-start.50 = (bf16[272,768]{1,0:T(8,128)(2,1)S(1)}, bf16[272,768]{1,0:T(8,128)(2,1)S(1)}, u32[]{:S(2)}, u32[]{:S(2)}) collective-permute-start(bf16[272,768]{1,0:T(8,128)(2,1)S(1)} %get-tuple-element.210.refs_0_.refs_12_.refs_6_), channel_id=1, source_target_pairs={{0,16},{16,0},{1,17},{17,1},{2,18},{18,2},{3,19},{19,3},{4,20},{20... | collective-permute-start | bytes 1253384 | tf_op jit(solution)/shard_map/ppermute | solution.py:148
  218.7 12.1 %collective-permute-start.51 = (bf16[272,768]{1,0:T(8,128)(2,1)S(1)}, bf16[272,768]{1,0:T(8,128)(2,1)S(1)}, u32[]{:S(2)}, u32[]{:S(2)}) collective-permute-start(bf16[272,768]{1,0:T(8,128)(2,1)S(1)} %get-tuple-element.210.refs_0_.refs_12_.refs_6_), channel_id=1, source_target_pairs={{0,1},{1,0},{2,3},{3,2},{4,5},{5,4},{6,7},{7,6},{8,9},{9,8},{10,11... | collective-permute-start | bytes 1253384 | tf_op jit(solution)/shard_map/ppermute | solution.py:152
  222.7 31.7 %collective-permute-start.64 = (bf16[768,1536]{1,0:T(8,128)(2,1)S(1)}, bf16[768,1536]{1,0:T(8,128)(2,1)S(1)}, u32[]{:S(2)}, u32[]{:S(2)}) collective-permute-start(bf16[768,1536]{1,0:T(8,128)(2,1)S(1)} %grads.4.refs_2_.refs_1_), channel_id=1, source_target_pairs={{2,0},{3,1},{16,18},{17,19},{6,4},{7,5},{20,22},{21,23},{10,8},{11... | collective-permute-start | bytes 7077896 | tf_op jit(solution)/shard_map/ppermute | solution.py:1298
  224.0 6.8 %collective-permute-start.43 = (bf16[272,768]{1,0:T(8,128)(2,1)S(1)}, bf16[272,768]{1,0:T(8,128)(2,1)S(1)}, u32[]{:S(2)}, u32[]{:S(2)}) collective-permute-start(bf16[272,768]{1,0:T(8,128)(2,1)S(1)} %get-tuple-element.198), channel_id=1, source_target_pairs={{0,16},{16,0},{1,17},{17,1},{2,18},{18,2},{3,19},{19,3},{4,20},{20... | collective-permute-start | bytes 1253384 | tf_op jit(solution)/shard_map/ppermute | solution.py:148
  231.0 15.3 %collective-permute-start.44 = (bf16[272,768]{1,0:T(8,128)(2,1)S(1)}, bf16[272,768]{1,0:T(8,128)(2,1)S(1)}, u32[]{:S(2)}, u32[]{:S(2)}) collective-permute-start(bf16[272,768]{1,0:T(8,128)(2,1)S(1)} %pair_sum.11.refs_7_), channel_id=1, source_target_pairs={{0,1},{1,0},{2,3},{3,2},{4,5},{5,4},{6,7},{7,6},{8,9},{9,8},{10,11... | collective-permute-start | bytes 1253384 | tf_op jit(solution)/shard_map/ppermute | solution.py:152
  249.1 11.2 %collective-permute-start.55 = (bf16[256,768]{1,0:T(8,128)(2,1)S(1)}, bf16[256,768]{1,0:T(8,128)(2,1)S(1)}, u32[]{:S(2)}, u32[]{:S(2)}) collective-permute-start(bf16[256,768]{1,0:T(8,128)(2,1)S(1)} %pair_sum.13.refs_6_.refs_12_), channel_id=1, source_target_pairs={{0,1},{1,0},{2,3},{3,2},{4,5},{5,4},{6,7},{7,6},{8,9},{9,8},{10,11... | collective-permute-start | bytes 1179656 | tf_op jit(solution)/shard_map/ppermute | solution.py:152
  251.2 9.2 %collective-permute-start.54 = (bf16[256,768]{1,0:T(8,128)(2,1)S(1)}, bf16[256,768]{1,0:T(8,128)(2,1)S(1)}, u32[]{:S(2)}, u32[]{:S(2)}) collective-permute-start(bf16[256,768]{1,0:T(8,128)(2,1)S(1)} %get-tuple-element.226), channel_id=1, source_target_pairs={{0,16},{16,0},{1,17},{17,1},{2,18},{18,2},{3,19},{19,3},{4,20},{20... | collective-permute-start | bytes 1179656 | tf_op jit(solution)/shard_map/ppermute | solution.py:148
  253.2 18.1 %collective-permute-start.62 = (bf16[768,768]{1,0:T(8,128)(2,1)S(1)}, bf16[768,768]{1,0:T(8,128)(2,1)S(1)}, u32[]{:S(2)}, u32[]{:S(2)}) collective-permute-start(bf16[768,768]{1,0:T(8,128)(2,1)S(1)} %grads.5.refs_2_.refs_10_.refs_1_), channel_id=1, source_target_pairs={{2,0},{3,1},{16,18},{17,19},{6,4},{7,5},{20,22},{21,23},{10,8},{11... | collective-permute-start | bytes 3538952 | tf_op jit(solution)/shard_map/ppermute | solution.py:1298
  255.6 18.1 %collective-permute-start.65 = (bf16[384,1536]{1,0:T(8,128)(2,1)S(1)}, bf16[384,1536]{1,0:T(8,128)(2,1)S(1)}, u32[]{:S(2)}, u32[]{:S(2)}) collective-permute-start(bf16[384,1536]{1,0:T(8,128)(2,1)S(1)} %get-tuple-element.242), channel_id=1, source_target_pairs={{0,4},{1,5},{18,22},{19,23},{4,0},{5,1},{22,18},{23,19},{8,12},{9,... | collective-permute-start | bytes 3538952 | tf_op jit(solution)/shard_map/ppermute | solution.py:1199
  261.5 12.1 %collective-permute-start.61 = (bf16[272,768]{1,0:T(8,128)(2,1)S(1)}, bf16[272,768]{1,0:T(8,128)(2,1)S(1)}, u32[]{:S(2)}, u32[]{:S(2)}) collective-permute-start(bf16[272,768]{1,0:T(8,128)(2,1)S(1)} %get-tuple-element.235.refs_0_.refs_6_), channel_id=1, source_target_pairs={{0,1},{1,0},{2,3},{3,2},{4,5},{5,4},{6,7},{7,6},{8,9},{9,8},{10,11... | collective-permute-start | bytes 1253384 | tf_op jit(solution)/shard_map/ppermute | solution.py:152
  263.3 20.6 %collective-permute-start.56 = (bf16[768,768]{1,0:T(8,128)(2,1)S(1)}, bf16[768,768]{1,0:T(8,128)(2,1)S(1)}, u32[]{:S(2)}, u32[]{:S(2)}) collective-permute-start(bf16[768,768]{1,0:T(8,128)(2,1)S(1)} %pack.1.refs_1_.refs_6_.refs_2_), channel_id=1, source_target_pairs={{2,0},{3,1},{16,18},{17,19},{6,4},{7,5},{20,22},{21,23},{10,8},{11... | collective-permute-start | bytes 3538952 | tf_op jit(solution)/shard_map/ppermute | solution.py:1433
  278.0 11.8 %collective-permute-start.68 = (bf16[384,768]{1,0:T(8,128)(2,1)S(1)}, bf16[384,768]{1,0:T(8,128)(2,1)S(1)}, u32[]{:S(2)}, u32[]{:S(2)}) collective-permute-start(bf16[384,768]{1,0:T(8,128)(2,1)S(1)} %get-tuple-element.249), channel_id=1, source_target_pairs={{0,4},{1,5},{18,22},{19,23},{4,0},{5,1},{22,18},{23,19},{8,12},{9,... | collective-permute-start | bytes 1769480 | tf_op jit(solution)/shard_map/ppermute | solution.py:1199
  281.2 8.7 %collective-permute-start.60 = (bf16[256,768]{1,0:T(8,128)(2,1)S(1)}, bf16[256,768]{1,0:T(8,128)(2,1)S(1)}, u32[]{:S(2)}, u32[]{:S(2)}) collective-permute-start(bf16[256,768]{1,0:T(8,128)(2,1)S(1)} %get-tuple-element.237), channel_id=1, source_target_pairs={{0,16},{16,0},{1,17},{17,1},{2,18},{18,2},{3,19},{19,3},{4,20},{20... | collective-permute-start | bytes 1179656 | tf_op jit(solution)/shard_map/ppermute | solution.py:148
  281.4 11.6 %collective-permute-start.67 = (bf16[256,768]{1,0:T(8,128)(2,1)S(1)}, bf16[256,768]{1,0:T(8,128)(2,1)S(1)}, u32[]{:S(2)}, u32[]{:S(2)}) collective-permute-start(bf16[256,768]{1,0:T(8,128)(2,1)S(1)} %pair_sum.14), channel_id=1, source_target_pairs={{0,1},{1,0},{2,3},{3,2},{4,5},{5,4},{6,7},{7,6},{8,9},{9,8},{10,11... | collective-permute-start | bytes 1179656 | tf_op jit(solution)/shard_map/ppermute | solution.py:152
  282.9 28.1 %collective-permute-start.57 = (bf16[768,768]{1,0:T(8,128)(2,1)S(1)}, bf16[768,768]{1,0:T(8,128)(2,1)S(1)}, u32[]{:S(2)}, u32[]{:S(2)}) collective-permute-start(bf16[768,768]{1,0:T(8,128)(2,1)S(1)} %pack.1.refs_1_.refs_6_.refs_2_), channel_id=1, source_target_pairs={{0,16},{16,0},{1,17},{17,1},{2,18},{18,2},{3,19},{19,3},{4,20},{20... | collective-permute-start | bytes 3538952 | tf_op jit(solution)/shard_map/ppermute | solution.py:148
  283.9 29.4 %collective-permute-start.58 = (bf16[768,768]{1,0:T(8,128)(2,1)S(1)}, bf16[768,768]{1,0:T(8,128)(2,1)S(1)}, u32[]{:S(2)}, u32[]{:S(2)}) collective-permute-start(bf16[768,768]{1,0:T(8,128)(2,1)S(1)} %collective-permute-done.56.refs_2_), channel_id=1, source_target_pairs={{0,16},{16,0},{1,17},{17,1},{2,18},{18,2},{3,19},{19,3},{4,20},{20... | collective-permute-start | bytes 3538952 | tf_op jit(solution)/shard_map/ppermute | solution.py:148
  294.2 12.1 %collective-permute-start.70 = (bf16[272,768]{1,0:T(8,128)(2,1)S(1)}, bf16[272,768]{1,0:T(8,128)(2,1)S(1)}, u32[]{:S(2)}, u32[]{:S(2)}) collective-permute-start(bf16[272,768]{1,0:T(8,128)(2,1)S(1)} %get-tuple-element.251.refs_0_.refs_12_.refs_6_), channel_id=1, source_target_pairs={{0,1},{1,0},{2,3},{3,2},{4,5},{5,4},{6,7},{7,6},{8,9},{9,8},{10,11... | collective-permute-start | bytes 1253384 | tf_op jit(solution)/shard_map/ppermute | solution.py:152
  298.5 39.2 %collective-permute-start.85 = (bf16[768,1536]{1,0:T(8,128)(2,1)S(1)}, bf16[768,1536]{1,0:T(8,128)(2,1)S(1)}, u32[]{:S(2)}, u32[]{:S(2)}) collective-permute-start(bf16[768,1536]{1,0:T(8,128)(2,1)S(1)} %grads.6.refs_2_.refs_1_), channel_id=1, source_target_pairs={{2,0},{3,1},{16,18},{17,19},{6,4},{7,5},{20,22},{21,23},{10,8},{11... | collective-permute-start | bytes 7077896 | tf_op jit(solution)/shard_map/ppermute | solution.py:1298
  306.3 8.6 %collective-permute-start.71 = (bf16[272,768]{1,0:T(8,128)(2,1)S(1)}, bf16[272,768]{1,0:T(8,128)(2,1)S(1)}, u32[]{:S(2)}, u32[]{:S(2)}) collective-permute-start(bf16[272,768]{1,0:T(8,128)(2,1)S(1)} %hold.28.refs_0_.refs_8_), channel_id=1, source_target_pairs={{0,16},{16,0},{1,17},{17,1},{2,18},{18,2},{3,19},{19,3},{4,20},{20... | collective-permute-start | bytes 1253384 | tf_op jit(solution)/shard_map/ppermute | solution.py:148
  306.4 23.2 %collective-permute-start.72 = (bf16[192,1536]{1,0:T(8,128)(2,1)S(1)}, bf16[192,1536]{1,0:T(8,128)(2,1)S(1)}, u32[]{:S(2)}, u32[]{:S(2)}) collective-permute-start(bf16[192,1536]{1,0:T(8,128)(2,1)S(1)} %get-tuple-element.263), channel_id=1, source_target_pairs={{0,8},{1,9},{18,26},{19,27},{4,12},{5,13},{22,30},{23,31},{8,0},{9... | collective-permute-start | bytes 1769480 | tf_op jit(solution)/shard_map/ppermute | solution.py:1199
  311.0 20.6 %collective-permute-start.73 = (bf16[192,768]{1,0:T(8,128)(2,1)S(1)}, bf16[192,768]{1,0:T(8,128)(2,1)S(1)}, u32[]{:S(2)}, u32[]{:S(2)}) collective-permute-start(bf16[192,768]{1,0:T(8,128)(2,1)S(1)} %get-tuple-element.264), channel_id=1, source_target_pairs={{0,8},{1,9},{18,26},{19,27},{4,12},{5,13},{22,30},{23,31},{8,0},{9... | collective-permute-start | bytes 884744 | tf_op jit(solution)/shard_map/ppermute | solution.py:1199
  336.4 20.9 %collective-permute-start.79 = (bf16[768,768]{1,0:T(8,128)(2,1)S(1)}, bf16[768,768]{1,0:T(8,128)(2,1)S(1)}, u32[]{:S(2)}, u32[]{:S(2)}) collective-permute-start(bf16[768,768]{1,0:T(8,128)(2,1)S(1)} %grads.7.refs_2_.refs_6_.refs_1_.refs_3_), channel_id=1, source_target_pairs={{2,0},{3,1},{16,18},{17,19},{6,4},{7,5},{20,22},{21,23},{10,8},{11... | collective-permute-start | bytes 3538952 | tf_op jit(solution)/shard_map/ppermute | solution.py:1298
  338.8 19.3 %collective-permute-start.86 = (bf16[384,1536]{1,0:T(8,128)(2,1)S(1)}, bf16[384,1536]{1,0:T(8,128)(2,1)S(1)}, u32[]{:S(2)}, u32[]{:S(2)}) collective-permute-start(bf16[384,1536]{1,0:T(8,128)(2,1)S(1)} %get-tuple-element.294), channel_id=1, source_target_pairs={{0,4},{1,5},{18,22},{19,23},{4,0},{5,1},{22,18},{23,19},{8,12},{9,... | collective-permute-start | bytes 3538952 | tf_op jit(solution)/shard_map/ppermute | solution.py:1199
  340.9 13.1 %collective-permute-start.76 = (bf16[256,768]{1,0:T(8,128)(2,1)S(1)}, bf16[256,768]{1,0:T(8,128)(2,1)S(1)}, u32[]{:S(2)}, u32[]{:S(2)}) collective-permute-start(bf16[256,768]{1,0:T(8,128)(2,1)S(1)} %pair_sum.15.refs_6_.refs_12_), channel_id=1, source_target_pairs={{0,1},{1,0},{2,3},{3,2},{4,5},{5,4},{6,7},{7,6},{8,9},{9,8},{10,11... | collective-permute-start | bytes 1179656 | tf_op jit(solution)/shard_map/ppermute | solution.py:152
  343.2 10.9 %collective-permute-start.75 = (bf16[256,768]{1,0:T(8,128)(2,1)S(1)}, bf16[256,768]{1,0:T(8,128)(2,1)S(1)}, u32[]{:S(2)}, u32[]{:S(2)}) collective-permute-start(bf16[256,768]{1,0:T(8,128)(2,1)S(1)} %get-tuple-element.268), channel_id=1, source_target_pairs={{0,16},{16,0},{1,17},{17,1},{2,18},{18,2},{3,19},{19,3},{4,20},{20... | collective-permute-start | bytes 1179656 | tf_op jit(solution)/shard_map/ppermute | solution.py:148
  345.1 8.2 %collective-permute-start.81 = (f32[8,768]{1,0:T(8,128)S(1)}, f32[8,768]{1,0:T(8,128)S(1)}, u32[]{:S(2)}, u32[]{:S(2)}) collective-permute-start(f32[8,768]{1,0:T(8,128)S(1)} %outer.1.refs_1_), channel_id=1, source_target_pairs={{0,1},{1,0},{2,3},{3,2},{4,5},{5,4},{6,7},{7,6},{8,9},{9,8},{10,11... | collective-permute-start | bytes 73736 | tf_op jit(solution)/shard_map/ppermute | solution.py:152
  358.5 18.9 %collective-permute-start.87 = (bf16[192,1536]{1,0:T(8,128)(2,1)S(1)}, bf16[192,1536]{1,0:T(8,128)(2,1)S(1)}, u32[]{:S(2)}, u32[]{:S(2)}) collective-permute-start(bf16[192,1536]{1,0:T(8,128)(2,1)S(1)} %get-tuple-element.296), channel_id=1, source_target_pairs={{0,8},{1,9},{18,26},{19,27},{4,12},{5,13},{22,30},{23,31},{8,0},{9... | collective-permute-start | bytes 1769480 | tf_op jit(solution)/shard_map/ppermute | solution.py:1199
  362.7 18.8 %collective-permute-start.83 = (bf16[432,768]{1,0:T(8,128)(2,1)S(1)}, bf16[432,768]{1,0:T(8,128)(2,1)S(1)}, u32[]{:S(2)}, u32[]{:S(2)}) collective-permute-start(bf16[432,768]{1,0:T(8,128)(2,1)S(1)} %get-tuple-element.288), channel_id=1, source_target_pairs={{0,4},{1,5},{18,22},{19,23},{4,0},{5,1},{22,18},{23,19},{8,12},{9,... | collective-permute-start | bytes 1990664 | tf_op jit(solution)/shard_map/ppermute | solution.py:1199
  365.3 24.2 %collective-permute-start.89 = (bf16[192,1536]{1,0:T(8,128)(2,1)S(1)}, bf16[192,1536]{1,0:T(8,128)(2,1)S(1)}, u32[]{:S(2)}, u32[]{:S(2)}) collective-permute-start(bf16[192,1536]{1,0:T(8,128)(2,1)S(1)} %total.3.refs_6_.refs_3_), channel_id=1, source_target_pairs={{0,16},{16,0},{1,17},{17,1},{2,18},{18,2},{3,19},{19,3},{4,20},{20... | collective-permute-start | bytes 1769480 | tf_op jit(solution)/shard_map/ppermute | solution.py:148
  377.5 12.0 %collective-permute-start.88 = (bf16[192,1536]{1,0:T(8,128)(2,1)S(1)}, bf16[192,1536]{1,0:T(8,128)(2,1)S(1)}, u32[]{:S(2)}, u32[]{:S(2)}) collective-permute-start(bf16[192,1536]{1,0:T(8,128)(2,1)S(1)} %total.5.refs_1_), channel_id=1, source_target_pairs={{0,16},{16,0},{1,17},{17,1},{2,18},{18,2},{3,19},{19,3},{4,20},{20... | collective-permute-start | bytes 1769480 | tf_op jit(solution)/shard_map/ppermute | solution.py:148
  378.2 9.7 %collective-permute-start.78 = (bf16[256,768]{1,0:T(8,128)(2,1)S(1)}, bf16[256,768]{1,0:T(8,128)(2,1)S(1)}, u32[]{:S(2)}, u32[]{:S(2)}) collective-permute-start(bf16[256,768]{1,0:T(8,128)(2,1)S(1)} %first_norm_back.3.refs_6_), channel_id=1, source_target_pairs={{2,0},{3,1},{18,2},{19,3},{6,4},{7,5},{22,6},{23,7},{10,8},{11,9},... | collective-permute-start | bytes 1179656 | tf_op jit(solution)/shard_map/ppermute | solution.py:1171
  381.6 13.2 %collective-permute-start.84 = (bf16[240,768]{1,0:T(8,128)(2,1)S(1)}, bf16[240,768]{1,0:T(8,128)(2,1)S(1)}, u32[]{:S(2)}, u32[]{:S(2)}) collective-permute-start(bf16[240,768]{1,0:T(8,128)(2,1)S(1)} %get-tuple-element.291), channel_id=1, source_target_pairs={{0,8},{1,9},{18,26},{19,27},{4,12},{5,13},{22,30},{23,31},{8,0},{9... | collective-permute-start | bytes 1105928 | tf_op jit(solution)/shard_map/ppermute | solution.py:1199
  383.6 13.0 %collective-permute-start.91 = (bf16[192,768]{1,0:T(8,128)(2,1)S(1)}, bf16[192,768]{1,0:T(8,128)(2,1)S(1)}, u32[]{:S(2)}, u32[]{:S(2)}) collective-permute-start(bf16[192,768]{1,0:T(8,128)(2,1)S(1)} %total.4.refs_7_.refs_5_.refs_3_), channel_id=1, source_target_pairs={{0,16},{16,0},{1,17},{17,1},{2,18},{18,2},{3,19},{19,3},{4,20},{20... | collective-permute-start | bytes 884744 | tf_op jit(solution)/shard_map/ppermute | solution.py:148
  (134 other events, 553.1 us)
Sparse Core Ops, SparseCore 0:
  26.4 47.5 all-gather.2
  91.8 29.8 all-gather.4
